TPU v7x, 128 devices: a whole 4x4x4 slice. The times are simulated.
128 devices in a mesh: fsdp: 16 (over z, x_hi, core), context: 4 (over y), tensor: 2 (over x_lo).
Axes of the slice: x: 4 (x_hi: 2, x_lo: 2; x = x_hi * 2 + x_lo), y: 4, z: 4, core: 2. Of those that a mesh axis runs over, the one named last changes fastest.
Arguments:
- tokens: bfloat16 [16384, 1536], P(('fsdp', 'context')), may hold values from -6 to 6
- cotangent: bfloat16 [16384, 1536], P(('fsdp', 'context')), may hold values from -6 to 6
- lengths: int32 [16, 3], P('fsdp'), may hold values from 1 to 896, 1024 in all within a row
- gain_attn: bfloat16 [1536], P('fsdp'), may hold values from 0.5 to 1.5
- w_query: bfloat16 [1536, 1536], P('fsdp', 'tensor'), may hold values from -0.15625 to 0.15625
- b_query: bfloat16 [1536], P('tensor'), may hold values from -3 to 3
- w_key: bfloat16 [1536, 256], P('fsdp', 'tensor'), may hold values from -0.15625 to 0.15625
- b_key: bfloat16 [256], P('tensor'), may hold values from -3 to 3
- w_value: bfloat16 [1536, 256], P('fsdp', 'tensor'), may hold values from -0.15625 to 0.15625
- b_value: bfloat16 [256], P('tensor'), may hold values from -3 to 3
- w_out: bfloat16 [1536, 1536], P('tensor', 'fsdp'), may hold values from -1.25 to 1.25
- gain_mlp: bfloat16 [1536], P('fsdp'), may hold values from 0.5 to 1.5
- w_gate: bfloat16 [1536, 8960], P('fsdp', 'tensor'), may hold values from -0.15625 to 0.15625
- w_up: bfloat16 [1536, 8960], P('fsdp', 'tensor'), may hold values from -0.15625 to 0.15625
- w_down: bfloat16 [8960, 1536], P('tensor', 'fsdp'), may hold values from -0.0625 to 0.0625
Outputs:
- result: bfloat16 [16384, 1536], P(('fsdp', 'context'))
- grad_tokens: float32 [16384, 1536], P(('fsdp', 'context'))
- grad_gain_attn: float32 [1536], P('fsdp')
- grad_w_query: float32 [1536, 1536], P('fsdp', 'tensor')
- grad_b_query: float32 [1536], P('tensor')
- grad_w_key: float32 [1536, 256], P('fsdp', 'tensor')
- grad_b_key: float32 [256], P('tensor')
- grad_w_value: float32 [1536, 256], P('fsdp', 'tensor')
- grad_b_value: float32 [256], P('tensor')
- grad_w_out: float32 [1536, 1536], P('tensor', 'fsdp')
- grad_gain_mlp: float32 [1536], P('fsdp')
- grad_w_gate: float32 [1536, 8960], P('fsdp', 'tensor')
- grad_w_up: float32 [1536, 8960], P('fsdp', 'tensor')
- grad_w_down: float32 [8960, 1536], P('tensor', 'fsdp')
Inputs may be any that keep to these rules, and one draw needn't show every extreme that they name: Each row holds the lengths of the 3 sequences packed in order into one group of 1024 tokens; they sum to 1024, and the longest is exactly 896.
All inputs are finite; a program needn't handle non-finite values.
Results may differ from a plain program's by a relative error of at most 0.024.
Values may be sent and summed in bfloat16 or wider, within the bound.
A program may use at most 320 MiB of HBM per device.

v0:
```python
import math

import jax
import jax.numpy as jnp
from jax import lax
from jax.sharding import PartitionSpec as P

HD = 128


ROPE_BASE = 1000000.0
EPSILON = 1e-06


def turned_gather(arrays, axis, dims):
    turned = [jnp.moveaxis(a, dim, 0) for a, dim in zip(arrays, dims)]
    both = jnp.concatenate([t.reshape(len(t), -1) for t in turned], axis=1)
    result, at, outs = (lax.all_gather(both, axis, axis=0, tiled=True), 0, [])
    for t, dim in zip(turned, dims):
        slab = result[:, at : at + t[0].size].reshape(-1, *t.shape[1:])
        outs.append(jnp.moveaxis(slab, 0, dim))
        at += t[0].size
    return tuple(outs)


def in_one_piece(arrays, axis, dim, along):
    both = jnp.concatenate(arrays, axis=along)
    result, at, outs = (lax.all_gather(both, axis, axis=dim, tiled=True), 0, [])
    for a in arrays:
        outs.append(lax.slice_in_dim(result, at, at + a.shape[along], axis=along))
        at += a.shape[along]
    return tuple(outs)


def from_everyone(x, axis):
    size = lax.axis_size(axis)
    return lax.all_to_all(jnp.broadcast_to(x[None], (size, *x.shape)), axis, 0, 0, tiled=True)


def over_copies(x, axis):
    return from_everyone(x, axis).sum(axis=0)


def of_everyone(x, axis):
    everything = from_everyone(x, axis)
    return jnp.sum(everything.astype(jnp.float32), axis=0)


def cut_along(x, dim, size):
    shape = x.shape
    tiles = x.reshape(*shape[:dim], size, shape[dim] // size, *shape[dim + 1 :])
    return jnp.moveaxis(tiles, dim, 0)


def summed_on_arrival(x, axis, dim):
    size = lax.axis_size(axis)
    tiles = lax.all_to_all(cut_along(x, dim, size), axis, 0, 0, tiled=True)
    return jnp.sum(tiles, axis=0)


def sent_together(arrays, axis, dim, along):
    both = jnp.concatenate(arrays, axis=along)
    result, at, outs = (summed_on_arrival(both, axis, dim), 0, [])
    for a in arrays:
        outs.append(lax.slice_in_dim(result, at, at + a.shape[along], axis=along))
        at += a.shape[along]
    return tuple(outs)


def in_one_piece_2(arrays, axis, dim, along):
    widths = [math.prod(a.shape[along:]) for a in arrays]
    both = jnp.concatenate(
        [a.reshape(*a.shape[:along], w) for a, w in zip(arrays, widths)], axis=along
    )
    result = lax.psum_scatter(both, axis, scatter_dimension=dim, tiled=True)
    tiles = jnp.split(result, [sum(widths[:k]) for k in range(1, len(widths))], axis=along)
    return tuple(
        (b.reshape(*result.shape[:along], *a.shape[along:]) for a, b in zip(arrays, tiles))
    )


def sent_together_2(arrays, axis, dim, along):
    widths = [a.shape[along] for a in arrays]
    both = jnp.concatenate(arrays, axis=along)
    result = lax.psum_scatter(both, axis, scatter_dimension=dim, tiled=True)
    return tuple(jnp.split(result, [sum(widths[:k]) for k in range(1, len(widths))], axis=along))


def for_sending(x):
    return jax.tree.map(lambda a: a.astype(jnp.bfloat16) if a.dtype == jnp.float32 else a, x)


def packed_total(arrays, axis):
    ends = [0]
    for a in arrays:
        ends.append(ends[-1] + a.size)
    total = over_copies(jnp.concatenate([a.ravel() for a in arrays]), axis)
    return tuple((total[b:e].reshape(a.shape) for a, b, e in zip(arrays, ends, ends[1:])))


def rms_norm(values, gain_vec):
    return (
        values * lax.rsqrt(jnp.mean(values * values, axis=-1, keepdims=True) + EPSILON) * gain_vec
    )


def rope_tables(positions, head_width):
    half_width = head_width // 2
    freq_index = jnp.arange(half_width).astype(jnp.float32)
    inverse = ROPE_BASE ** (-(freq_index * 2.0 / head_width))
    angles = positions.astype(jnp.float32)[:, None] * inverse[None, :]
    cosine = jnp.cos(angles)
    sine_table = jnp.sin(angles)
    return (jnp.concatenate([cosine, cosine], -1), jnp.concatenate([sine_table, sine_table], -1))


def rotate(values, cosine, sine_table):
    half_width = values.shape[-1] // 2
    turned = jnp.concatenate([-values[..., half_width:], values[..., :half_width]], -1)
    return values * cosine[:, None, :] + turned * sine_table[:, None, :]


def segment_info(seq_lengths, total_rows):
    ends_at = jnp.cumsum(seq_lengths)
    places = jnp.arange(total_rows, dtype=jnp.int32)
    passed = places[:, None] >= ends_at[None, :]
    segment = jnp.sum(passed.astype(jnp.int32), axis=1)
    starts = jnp.sum(jnp.where(passed, seq_lengths[None, :], 0), axis=1)
    return (segment, places - starts)


def lead_dot(left, right):
    return lax.dot_general(
        left, right, (((0,), (0,)), ((), ())), preferred_element_type=jnp.float32
    )


def tail_dot(left, right):
    return lax.dot_general(
        left, right, (((1,), (1,)), ((), ())), preferred_element_type=jnp.float32
    )


def fetch(gain_attn, gain_mlp, w_query, w_key, w_value, w_gate, w_up, w_out, w_down):
    row_part = turned_gather(
        (gain_attn, gain_mlp, w_query, w_key, w_value, w_gate, w_up), "fsdp", (0, 0, 0, 0, 0, 0, 0)
    )
    col_part = turned_gather((w_out, w_down), "fsdp", (1, 1))
    return tuple(row_part) + tuple(col_part)


def on_device(
    tokens,
    cotangent,
    lengths,
    gain_attn,
    w_query,
    b_query,
    w_key,
    b_key,
    w_value,
    b_value,
    w_out,
    gain_mlp,
    w_gate,
    w_up,
    w_down,
):
    row_count = tokens.shape[0]
    context_size = lax.axis_size("context")
    context_rank = lax.axis_index("context")
    heads_kv = w_key.shape[1] // HD
    heads_query = w_query.shape[1] // HD
    per_group = heads_query // heads_kv
    score_scale = HD ** (-0.5)
    group_rows = row_count * context_size
    segment_all, position_all = segment_info(lengths[0], group_rows)
    first_row = context_rank * row_count
    segment_mine = lax.dynamic_slice_in_dim(segment_all, first_row, row_count)
    position_mine = lax.dynamic_slice_in_dim(position_all, first_row, row_count)
    query_at = first_row + jnp.arange(row_count, dtype=jnp.int32)
    key_at = jnp.arange(group_rows, dtype=jnp.int32)
    allowed = (segment_mine[:, None] == segment_all[None, :]) & (
        key_at[None, :] <= query_at[:, None]
    )
    cosine, sine_table = rope_tables(position_mine, HD)
    fetched = fetch(gain_attn, gain_mlp, w_query, w_key, w_value, w_gate, w_up, w_out, w_down)
    gain_one = fetched[0].astype(jnp.float32)
    gain_two = fetched[1].astype(jnp.float32)
    query_full, key_full, value_full, gate_full, lift_full, out_full, down_full = fetched[2:]
    inputs = tokens.astype(jnp.float32)
    normed_one = rms_norm(inputs, gain_one).astype(jnp.bfloat16)
    query_lin = jnp.dot(
        normed_one, query_full, preferred_element_type=jnp.float32
    ) + b_query.astype(jnp.float32)
    key_lin = jnp.dot(normed_one, key_full, preferred_element_type=jnp.float32) + b_key.astype(
        jnp.float32
    )
    value_lin = jnp.dot(
        normed_one, value_full, preferred_element_type=jnp.float32
    ) + b_value.astype(jnp.float32)
    query_heads = rotate(query_lin.reshape(row_count, heads_query, HD), cosine, sine_table).astype(
        jnp.bfloat16
    )
    query_heads = query_heads.reshape(row_count, heads_kv, per_group, HD)
    key_heads = rotate(key_lin.reshape(row_count, heads_kv, HD), cosine, sine_table).astype(
        jnp.bfloat16
    )
    value_heads = value_lin.astype(jnp.bfloat16).reshape(row_count, heads_kv, HD)
    key_group, value_group = in_one_piece((key_heads, value_heads), "context", 0, 1)
    scores = (
        jnp.einsum("qgjd,kgd->gjqk", query_heads, key_group, preferred_element_type=jnp.float32)
        * score_scale
    )
    scores = jnp.where(allowed, scores, -1e30)
    row_top = jnp.max(scores, axis=-1, keepdims=True)
    expo = jnp.exp(scores - row_top)
    probs = expo / jnp.sum(expo, axis=-1, keepdims=True)
    probs_low = probs.astype(jnp.bfloat16)
    mixed = jnp.einsum("gjqk,kgd->qgjd", probs_low, value_group, preferred_element_type=jnp.float32)
    mixed = mixed.reshape(row_count, heads_query * HD).astype(jnp.bfloat16)
    attn_branch = over_copies(
        jnp.dot(mixed, out_full, preferred_element_type=jnp.float32), "tensor"
    )
    middle = inputs + attn_branch
    normed_two = rms_norm(middle, gain_two).astype(jnp.bfloat16)
    gate_lin = jnp.dot(normed_two, gate_full, preferred_element_type=jnp.float32)
    lift_lin = jnp.dot(normed_two, lift_full, preferred_element_type=jnp.float32)
    sigmoid_gate = jax.nn.sigmoid(gate_lin)
    swish = gate_lin * sigmoid_gate
    hidden = (swish * lift_lin).astype(jnp.bfloat16)
    mlp_branch = of_everyone(
        jnp.dot(hidden, down_full, preferred_element_type=jnp.float32).astype(jnp.bfloat16),
        "tensor",
    ).astype(jnp.float32)
    result = (middle + mlp_branch).astype(jnp.bfloat16)
    fetched = fetch(gain_attn, gain_mlp, w_query, w_key, w_value, w_gate, w_up, w_out, w_down)
    query_full, key_full, value_full, gate_full, lift_full, out_full, down_full = fetched[2:]
    d_hidden = tail_dot(cotangent, down_full)
    grad_w_down = lead_dot(hidden, cotangent)
    d_gate = (d_hidden * lift_lin * sigmoid_gate * (1.0 + gate_lin * (1.0 - sigmoid_gate))).astype(
        jnp.bfloat16
    )
    d_lift = (d_hidden * swish).astype(jnp.bfloat16)
    grad_w_gate = lead_dot(normed_two, d_gate)
    grad_w_up = lead_dot(normed_two, d_lift)
    d_normed_two = over_copies(tail_dot(d_gate, gate_full) + tail_dot(d_lift, lift_full), "tensor")
    _, pull_two = jax.vjp(rms_norm, middle, gain_two)
    d_middle_norm, grad_gain_mlp = pull_two(d_normed_two)
    d_middle = cotangent.astype(jnp.float32) + d_middle_norm
    d_branch = d_middle.astype(jnp.bfloat16)
    grad_w_out = lead_dot(mixed, d_branch)
    d_mixed = (
        tail_dot(d_branch, out_full)
        .astype(jnp.bfloat16)
        .reshape(row_count, heads_kv, per_group, HD)
    )
    d_probs = jnp.einsum("qgjd,kgd->gjqk", d_mixed, value_group, preferred_element_type=jnp.float32)
    inner = jnp.sum(probs * d_probs, axis=-1, keepdims=True)
    d_scores = (probs * (d_probs - inner)).astype(jnp.bfloat16)
    d_query = (
        jnp.einsum("gjqk,kgd->qgjd", d_scores, key_group, preferred_element_type=jnp.float32)
        * score_scale
    )
    d_key_part = (
        jnp.einsum("gjqk,qgjd->kgd", d_scores, query_heads, preferred_element_type=jnp.float32)
        * score_scale
    )
    d_value_part = jnp.einsum(
        "gjqk,qgjd->kgd", probs_low, d_mixed, preferred_element_type=jnp.float32
    )
    d_key, d_value = sent_together((d_key_part, d_value_part), "context", 0, 1)

    def turn_query(values):
        return rotate(values, cosine, sine_table)

    _, pull_query = jax.vjp(turn_query, query_lin.reshape(row_count, heads_query, HD))
    _, pull_key = jax.vjp(turn_query, key_lin.reshape(row_count, heads_kv, HD))
    d_query_lin = (
        pull_query(d_query.reshape(row_count, heads_query, HD))[0]
        .reshape(row_count, heads_query * HD)
        .astype(jnp.bfloat16)
    )
    d_key_lin = pull_key(d_key)[0].reshape(row_count, heads_kv * HD).astype(jnp.bfloat16)
    d_value_lin = d_value.reshape(row_count, heads_kv * HD).astype(jnp.bfloat16)
    bias_query = jnp.sum(d_query_lin.astype(jnp.float32), axis=0)
    bias_key = jnp.sum(d_key_lin.astype(jnp.float32), axis=0)
    bias_value = jnp.sum(d_value_lin.astype(jnp.float32), axis=0)
    grad_w_query = lead_dot(normed_one, d_query_lin)
    grad_w_key = lead_dot(normed_one, d_key_lin)
    grad_w_value = lead_dot(normed_one, d_value_lin)
    d_normed_part = (
        tail_dot(d_query_lin, query_full)
        + tail_dot(d_key_lin, key_full)
        + tail_dot(d_value_lin, value_full)
    )
    d_normed_one = of_everyone(d_normed_part.astype(jnp.bfloat16), "tensor").astype(jnp.float32)
    _, pull_one = jax.vjp(rms_norm, inputs, gain_one)
    d_input_norm, grad_gain_attn = pull_one(d_normed_one)
    grad_tokens = d_middle + d_input_norm
    row_grads = (
        lax.psum_scatter(
            grad_gain_attn.astype(jnp.bfloat16), "fsdp", scatter_dimension=0, tiled=True
        ).astype(jnp.float32),
        *tuple(
            (
                part.astype(jnp.float32)
                for part in in_one_piece_2(
                    (
                        grad_gain_mlp.astype(jnp.bfloat16),
                        grad_w_query.astype(jnp.bfloat16),
                        grad_w_key.astype(jnp.bfloat16),
                        grad_w_value.astype(jnp.bfloat16),
                        grad_w_gate.astype(jnp.bfloat16),
                        grad_w_up.astype(jnp.bfloat16),
                    ),
                    "fsdp",
                    0,
                    1,
                )
            )
        ),
    )
    col_grads = tuple(
        (
            part.astype(jnp.float32)
            for part in sent_together_2(
                (grad_w_out.astype(jnp.bfloat16), grad_w_down.astype(jnp.bfloat16)), "fsdp", 1, 0
            )
        )
    )
    summed = jax.tree.map(
        lambda part: part.astype(jnp.float32),
        lax.psum(for_sending(tuple(row_grads) + tuple(col_grads)), "context"),
    )
    bias_grads = packed_total((bias_query, bias_key, bias_value), ("fsdp", "context"))
    return (
        result,
        grad_tokens,
        summed[0],
        summed[2],
        bias_grads[0],
        summed[3],
        bias_grads[1],
        summed[4],
        bias_grads[2],
        summed[7],
        summed[1],
        summed[5],
        summed[6],
        summed[8],
    )


def solution(mesh):
    return jax.shard_map(
        on_device,
        mesh=mesh,
        in_specs=(
            P(("fsdp", "context"), None),
            P(("fsdp", "context"), None),
            P("fsdp", None),
            P("fsdp"),
            P("fsdp", "tensor"),
            P("tensor"),
            P("fsdp", "tensor"),
            P("tensor"),
            P("fsdp", "tensor"),
            P("tensor"),
            P("tensor", "fsdp"),
            P("fsdp"),
            P("fsdp", "tensor"),
            P("fsdp", "tensor"),
            P("tensor", "fsdp"),
        ),
        out_specs=(
            P(("fsdp", "context"), None),
            P(("fsdp", "context"), None),
            P("fsdp"),
            P("fsdp", "tensor"),
            P("tensor"),
            P("fsdp", "tensor"),
            P("tensor"),
            P("fsdp", "tensor"),
            P("tensor"),
            P("tensor", "fsdp"),
            P("fsdp"),
            P("fsdp", "tensor"),
            P("fsdp", "tensor"),
            P("tensor", "fsdp"),
        ),
        check_vma=False,
    )
```

profile of v0, /device:TPU:0, one launch (start us, length us, event | category | flops | bytes accessed | tf_op | source)
XLA Modules:
  0.0 980.7 jit_solution(16332296934652553109)
XLA Ops:
  8.8 4.7 concatenate.43
  16.5 174.4 %all-gather.3.cloned.1.call-done = bf16[1536,9986]{1,0:T(8,128)(2,1)} async-done(((bf16[96,9986]{1,0:T(8,128)(2,1)}), bf16[1536,9986]{1,0:T(8,128)(2,1)}) %all-gather.3.cloned.1.call-update) | async-done | bytes 30677008 | tf_op jit(solution)/shard_map/all_gather | solution.py:18
  191.0 1.6 convert_reduce_fusion.2
  192.6 3.0 fusion.51
  195.9 2.0 convolution_add_fusion.3
  201.6 1.7 add_convert_fusion.3
  203.5 1.8 fusion.67
  205.3 13.2 %all_gather.12 = bf16[1024,2,128]{0,2,1:T(8,128)(2,1)S(1)} all-gather(bf16[256,2,128]{0,2,1:T(8,128)(2,1)S(1)} %pad_maximum_fusion.5), channel_id=1, replica_groups=mesh['fsdp'=16,'context'=4,'tensor'=2] {'context'}, dimensions={0}, use_global_device_ids=true | all-gather | bytes 655360 | tf_op jit(solution)/shard_map/all_gather | solution.py:28
  222.3 1.9 fusion.58
  224.2 73.6 %all-gather.5.cloned.1.call-done = bf16[1536,5248]{1,0:T(8,128)(2,1)} async-done(((bf16[96,5248]{1,0:T(8,128)(2,1)}), bf16[1536,5248]{1,0:T(8,128)(2,1)}) %all-gather.5.cloned.1.call-update) | async-done | bytes 16121872 | tf_op jit(solution)/shard_map/all_gather | solution.py:18
  297.9 2.5 fusion.37
  300.4 2.0 broadcast_in_dim.45
  302.4 5.5 all-to-all-start
  307.9 10.8 %fusion.12 = f32[256,4480]{1,0:T(8,128)} fusion(bf16[256,1536]{1,0:T(8,128)(2,1)S(1)} %copy-done.16, bf16[1536,5248]{1,0:T(8,128)(2,1)} %all-gather.5.cloned.1.call-done), kind=kOutput, calls=%fused_computation.16 | convolution fusion | flops 3523215360 | bytes 19136512 | tf_op jit(solution)/shard_map/dot_general | solution.py:139
  318.7 26.0 %all-to-all-done = f32[2,256,1536]{2,1,0:T(8,128)} async-done(((f32[2,256,1536]{2,1,0:T(8,128)}), f32[2,256,1536]{2,1,0:T(8,128)}, u32[]{:S(2)}, u32[]{:S(2)}) %all-to-all-start) | async-done | bytes 3145760 | tf_op jit(solution)/shard_map/all_to_all | solution.py:37
  344.8 3.4 reduce_sum.201
  348.2 1.7 multiply_reduce_fusion.2
  350.1 12.1 %fusion.6 = f32[256,4480]{1,0:T(8,128)} fusion(bf16[256,1536]{1,0:T(8,128)(2,1)S(1)} %multiply_convert_fusion.3, bf16[1536,9986]{1,0:T(8,128)(2,1)} %all-gather.3.cloned.1.call-done), kind=kOutput, calls=%fused_computation.10 | convolution fusion | flops 3523215360 | bytes 19136512 | tf_op jit(solution)/shard_map/dot_general | solution.py:228
  362.2 13.6 %multiply_convert_fusion.1 = (bf16[256,4480]{1,0:T(8,128)(2,1)}, bf16[256,4480]{1,0:T(8,128)(2,1)}, bf16[256,4480]{1,0:T(8,128)(2,1)S(1)}) fusion(f32[256,4480]{1,0:T(8,128)} %fusion.12, f32[256,4480]{1,0:T(8,128)} %fusion.6, bf16[256,1536]{1,0:T(8,128)(2,1)S(1)} %multiply_convert_fusion.3, bf16[1536,9986]{1,0:T(8,128)(2,1)} %all-gather.3.cloned.1.call-done), kind=kOutput, calls=%fused_computation.28 | convolution fusion | flops 3540418560 | bytes 30605312 | tf_op jit(solution)/shard_map/dot_general | solution.py:227
  375.8 9.6 fusion.30
  386.6 3.7 all-to-all-start.1
  390.3 9.7 fusion.4
  400.0 11.5 %fusion.27 = f32[256,1536]{1,0:T(8,128)} fusion(f32[256,1536]{1,0:T(8,128)S(1)} %fusion.4, bf16[256,4480]{1,0:T(8,128)(2,1)S(1)} %copy-done.18, bf16[1536,9986]{1,0:T(8,128)(2,1)} %all-gather.3.cloned.1.call-done), kind=kOutput, calls=%fused_computation.48 | convolution fusion | flops 3523608576 | bytes 19202048 | tf_op jit(solution)/shard_map/dot_general | solution.py:139
  411.5 3.4 broadcast_in_dim.47
  415.0 5.2 all-to-all-start.2
  420.4 10.5 %convolution_convert_fusion = bf16[4480,1536]{1,0:T(8,128)(2,1)} fusion(bf16[256,4480]{1,0:T(8,128)(2,1)} %copy-done.15, bf16[256,1536]{1,0:T(8,128)(2,1)} %param.16), kind=kOutput, calls=%fused_computation | convolution fusion | flops 3530096640 | bytes 16842752 | tf_op jit(solution)/shard_map/dot_general | solution.py:133
  432.3 24.0 %all-to-all-done.2 = f32[2,256,1536]{2,1,0:T(8,128)} async-done(((f32[2,256,1536]{2,1,0:T(8,128)}), f32[2,256,1536]{2,1,0:T(8,128)}, u32[]{:S(2)}, u32[]{:S(2)}) %all-to-all-start.2) | async-done | bytes 3145760 | tf_op jit(solution)/shard_map/all_to_all | solution.py:37
  456.2 2.3 reduce_sum.204
  459.5 3.4 fusion.47
  464.0 1.8 convolution_convert_fusion.4
  465.8 12.3 %pad_maximum_fusion = bf16[5248,1536]{1,0:T(8,128)(2,1)} fusion(bf16[4480,1536]{1,0:T(8,128)(2,1)S(1)} %copy-done, bf16[768,1536]{1,0:T(8,128)(2,1)S(1)} %convolution_convert_fusion.4), kind=kLoop, calls=%fused_computation.3 | loop fusion | flops 32243712 | bytes 32243712 | tf_op jit(solution)/shard_map/concatenate | solution.py:84
  478.1 20.5 %copy.160 = bf16[5248,1536]{0,1:T(8,128)(2,1)} copy(bf16[5248,1536]{1,0:T(8,128)(2,1)} %pad_maximum_fusion) | data formatting | bytes 32243712
  499.7 10.7 %convolution_convert_fusion.2 = bf16[1536,4480]{1,0:T(8,128)(2,1)} fusion(bf16[256,1536]{1,0:T(8,128)(2,1)S(1)} %copy-done.10, bf16[256,4480]{1,0:T(8,128)(2,1)} %get-tuple-element.107), kind=kOutput, calls=%fused_computation.2 | convolution fusion | flops 3530096640 | bytes 16842752 | tf_op jit(solution)/shard_map/dot_general | solution.py:133
  510.4 9.0 convolution_convert_fusion.1
  519.4 3.0 fusion.55
  522.6 5.0 fusion.15
  528.5 2.8 fusion.22
  532.5 2.0 fusion.61
  535.8 4.3 all-to-all-start.3
  541.4 1.6 broadcast_multiply_fusion
  545.1 2.5 copy.142
  547.5 6.3 all-to-all-done.3
  557.1 2.0 copy.143
  560.2 1.9 copy.144
  562.1 56.5 %concatenate.53 = bf16[1536,9985]{1,0:T(8,128)(2,1)} concatenate(bf16[1536,1]{1,0:T(8,128)(2,1)} %convert_element_type.296, bf16[1536,768]{1,0:T(8,128)(2,1)S(1)} %copy-done.8, bf16[1536,128]{1,0:T(8,128)(2,1)} %copy.143, bf16[1536,128]{1,0:T(8,128)(2,1)} %copy.144, bf16[1536,4480]{1,0:T(8,128)(2,1)} %convolution_convert_fusion.2, bf16[1536,4480]{1,0:T(8,128)(2,1)} %convolution_convert_fusion.1), dimensions={1} | concatenate | bytes 61347840 | tf_op jit(solution)/shard_map/concatenate | solution.py:72
  619.7 4.4 fusion.39
  624.9 4.7 all-to-all-start.5
  629.7 13.2 %reduce-scatter.7.cloned.1.call-done = bf16[96,5248]{1,0:T(8,128)(2,1)} async-done(((bf16[1536,5248]{1,0:T(8,128)(2,1)}), bf16[96,5248]{1,0:T(8,128)(2,1)}) %reduce-scatter.7.cloned.1.call-update) | async-done | bytes 1007632
  645.9 1.4 copy.167
  647.3 221.1 %reduce-scatter.5.cloned.1.call-done = bf16[96,9985]{1,0:T(8,128)(2,1)} async-done(((bf16[1536,9985]{1,0:T(8,128)(2,1)}), bf16[96,9985]{1,0:T(8,128)(2,1)}) %reduce-scatter.5.cloned.1.call-update) | async-done | bytes 1917136 | tf_op jit(solution)/shard_map/reduce_scatter | solution.py:75
  868.4 1.7 split.52
  870.1 3.2 fusion.100
  874.7 1.7 convolution_add_fusion.1
  876.4 1.7 fusion.33
  879.3 4.6 all-to-all-start.4
  885.9 17.0 %all-to-all-done.4 = bf16[2,256,1536]{2,1,0:T(8,128)(2,1)} async-done(((bf16[2,256,1536]{2,1,0:T(8,128)(2,1)}), bf16[2,256,1536]{2,1,0:T(8,128)(2,1)}, u32[]{:S(2)}, u32[]{:S(2)}) %all-to-all-start.4) | async-done | bytes 1572896 | tf_op jit(solution)/shard_map/all_to_all | solution.py:37
  903.0 1.9 convert_reduce_fusion
  906.5 33.2 %all-reduce.4 = bf16[1536]{0:T(1024)(128)(2,1)S(1)} all-reduce(bf16[1536]{0:T(1024)(128)(2,1)S(1)} %get-tuple-element.88), channel_id=2, replica_groups=mesh['fsdp'=16,'context'=4,'tensor'=2] {'fsdp'}, use_global_device_ids=true, to_apply=%region_16.17.clone | all-reduce | flops 1536 | bytes 6144
  939.8 3.0 fusion.48
  944.6 17.5 %all-reduce.5 = (bf16[96]{0:T(256)(128)(2,1)S(1)}, bf16[96,128]{1,0:T(8,128)(2,1)S(1)}, bf16[96,128]{1,0:T(8,128)(2,1)S(1)}, bf16[96]{0:T(256)(128)(2,1)S(1)}) all-reduce(bf16[96]{0:T(256)(128)(2,1)S(1)} %dynamic-slice.1, bf16[96,128]{1,0:T(8,128)(2,1)S(1)} %get-tuple-element.113, ...), channel_id=1, replica_groups=mesh['fsdp'=16,'context'=4,'tensor'=2] {'context'}, use_global_device_ids=true, to_apply=%region_17.18 | all-reduce | flops 24768 | bytes 99072 | tf_op jit(solution)/shard_map/psum | solution.py:334
  964.4 1.7 convert_element_type.281
  966.2 1.8 copy.146
  967.9 2.6 convert_element_type.291
  971.8 1.9 copy.147
  (200 shorter events, 45.8 us)
Async XLA Ops:
  7.2 183.8 %all-gather.3.cloned.1.call-start = ((), (), s32[]{:S(2)}) async-start(), calls=%async_computation.8 | async-start | bytes 33005568 | tf_op jit(solution)/shard_map/all_gather | solution.py:18
  8.8 4.9 copy-start.30
  8.8 4.9 copy-start.39
  13.5 1.2 copy-start.54
  13.5 1.7 copy-start.53
  13.5 1.9 copy-start.55
  13.5 1.9 copy-start.52
  13.5 2.2 copy-start.2
  13.6 284.3 %all-gather.5.cloned.1.call-start = ((), (), s32[]{:S(2)}) async-start(), calls=%async_computation.9 | async-start | bytes 17129472 | tf_op jit(solution)/shard_map/all_gather | solution.py:18
  15.9 179.6 %copy-start.47 = (f32[256]{0:T(256)}, f32[256]{0:T(256)S(1)}, u32[]{:S(2)}) copy-start(f32[256]{0:T(256)S(1)} %fusion.49) | copy-start | bytes 3076
  15.9 179.9 %copy-start.45 = (f32[256]{0:T(256)}, f32[256]{0:T(256)S(1)}, u32[]{:S(2)}) copy-start(f32[256]{0:T(256)S(1)} %fusion.87) | copy-start | bytes 3076
  16.3 181.7 %copy-start.31 = (f32[256,64]{0,1:T(8,128)}, f32[256,64]{0,1:T(8,128)S(1)}, u32[]{:S(2)}) copy-start(f32[256,64]{0,1:T(8,128)S(1)} %get-tuple-element.130) | copy-start | bytes 196612
  16.3 181.7 %copy-start.33 = (f32[256,64]{0,1:T(8,128)}, f32[256,64]{0,1:T(8,128)S(1)}, u32[]{:S(2)}) copy-start(f32[256,64]{0,1:T(8,128)S(1)} %get-tuple-element.131) | copy-start | bytes 196612
  192.6 10.9 %copy-start.40 = (f32[1536]{0:T(1024)}, f32[1536]{0:T(1024)S(1)}, u32[]{:S(2)}) copy-start(f32[1536]{0:T(1024)S(1)} %get-tuple-element.85) | copy-start | bytes 18436
  195.9 2.9 copy-start.11
  198.6 1.8 copy-start.21
  199.3 4.0 copy-start.13
  201.6 3.6 copy-start.38
  218.5 2.5 copy-start.19
  219.6 2.6 copy-start.1
  222.3 300.3 %copy-start.42 = (f32[6,256]{1,0:T(8,128)}, f32[6,256]{1,0:T(8,128)S(1)}, u32[]{:S(2)}) copy-start(f32[6,256]{1,0:T(8,128)S(1)} %fusion.19) | copy-start | bytes 18436
  224.2 78.2 %copy-start.35 = (bf16[128,6,256]{2,0,1:T(8,128)(2,1)}, bf16[128,6,256]{2,0,1:T(8,128)(2,1)S(1)}, u32[]{:S(2)}) copy-start(bf16[128,6,256]{2,0,1:T(8,128)(2,1)S(1)} %fusion.58) | copy-start | bytes 1179652
  302.4 5.5 copy-start.16
  302.4 42.4 %all-to-all-start = ((f32[2,256,1536]{2,1,0:T(8,128)}), f32[2,256,1536]{2,1,0:T(8,128)}, u32[]{:S(2)}, u32[]{:S(2)}) async-start(f32[2,256,1536]{2,1,0:T(8,128)} %broadcast_in_dim.45), calls=%async_computation | async-start | bytes 6291456 | tf_op jit(solution)/shard_map/all_to_all | solution.py:37
  350.1 12.1 %copy-start.9 = (bf16[256,1536]{1,0:T(8,128)(2,1)}, bf16[256,1536]{1,0:T(8,128)(2,1)S(1)}, u32[]{:S(2)}) copy-start(bf16[256,1536]{1,0:T(8,128)(2,1)S(1)} %multiply_convert_fusion.3) | copy-start | bytes 2359300
  375.8 9.6 copy-start.15
  386.6 24.9 %all-to-all-start.1 = ((bf16[2,256,1536]{2,1,0:T(8,128)(2,1)}), bf16[2,256,1536]{2,1,0:T(8,128)(2,1)S(1)}, u32[]{:S(2)}, u32[]{:S(2)}) async-start(bf16[2,256,1536]{2,1,0:T(8,128)(2,1)} %broadcast_in_dim.46), calls=%async_computation.1 | async-start | bytes 3145728 | tf_op jit(solution)/shard_map/all_to_all | solution.py:37
  390.3 9.7 copy-start.18
  415.0 41.3 %all-to-all-start.2 = ((f32[2,256,1536]{2,1,0:T(8,128)}), f32[2,256,1536]{2,1,0:T(8,128)}, u32[]{:S(2)}, u32[]{:S(2)}) async-start(f32[2,256,1536]{2,1,0:T(8,128)} %broadcast_in_dim.47), calls=%async_computation.2 | async-start | bytes 6291456 | tf_op jit(solution)/shard_map/all_to_all | solution.py:37
  420.2 222.7 %reduce-scatter.7.cloned.1.call-start = ((), (), s32[]{:S(2)}) async-start(), calls=%async_computation.11 | async-start | bytes 17129472
  458.5 7.3 copy-start
  462.9 1.1 copy-start.4
  499.7 10.7 %copy-start.17 = (bf16[256,4480]{1,0:T(8,128)(2,1)S(1)}, bf16[256,4480]{1,0:T(8,128)(2,1)}, u32[]{:S(2)}) copy-start(bf16[256,4480]{1,0:T(8,128)(2,1)} %get-tuple-element.108) | copy-start | bytes 6881284
  510.4 9.0 copy-start.5
  519.4 3.2 copy-start.20
  522.6 5.1 copy-start.36
  522.6 5.2 slice-start
  522.6 5.9 slice-start.1
  528.5 2.8 copy-start.12
  528.5 2.8 copy-start.14
  528.5 2.8 copy-start.22
  531.3 1.2 copy-start.37
  531.3 1.2 copy-start.43
  534.7 5.7 copy-start.44
  534.7 6.7 copy-start.27
  535.8 18.0 %all-to-all-start.3 = ((f32[4,256,2,128]{1,3,2,0:T(8,128)}), f32[4,256,2,128]{1,3,2,0:T(8,128)}, u32[]{:S(2)}, u32[]{:S(2)}) async-start(f32[4,256,2,128]{1,3,2,0:T(8,128)} %bitcast.176), calls=%async_computation.3 | async-start | bytes 2097152 | tf_op jit(solution)/shard_map/all_to_all | solution.py:57
  540.1 328.3 %reduce-scatter.5.cloned.1.call-start = ((), (), s32[]{:S(2)}) async-start(), calls=%async_computation.10 | async-start | bytes 33005568 | tf_op jit(solution)/shard_map/reduce_scatter | solution.py:75
  543.0 1.1 copy-start.3
  545.1 10.1 %copy-start.34 = (f32[256,64]{0,1:T(8,128)S(1)}, f32[256,64]{0,1:T(8,128)}, u32[]{:S(2)}) copy-start(f32[256,64]{0,1:T(8,128)} %copy-done.33) | copy-start | bytes 196612
  545.1 10.2 %copy-start.32 = (f32[256,64]{0,1:T(8,128)S(1)}, f32[256,64]{0,1:T(8,128)}, u32[]{:S(2)}) copy-start(f32[256,64]{0,1:T(8,128)} %copy-done.31) | copy-start | bytes 196612
  555.9 6.2 copy-start.8
  619.6 4.4 copy-start.50
  619.7 4.4 copy-start.51
  624.9 253.1 %all-to-all-start.5 = ((f32[64,1,1024]{2,1,0:T(1,128)}), f32[64,1,1024]{2,1,0:T(1,128)S(1)}, u32[]{:S(2)}, u32[]{:S(2)}) async-start(f32[64,1,1024]{2,1,0:T(1,128)} %broadcast_in_dim.53), calls=%async_computation.6 | async-start | bytes 524288 | tf_op jit(solution)/shard_map/all_to_all | solution.py:37
  629.6 334.8 %all-reduce.9.cloned.1.call-start = ((), (), s32[]{:S(2)}) async-start(), calls=%async_computation.12 | async-start | bytes 6422528 | tf_op jit(solution)/shard_map/psum | solution.py:334
  873.3 1.4 copy-start.23
  878.1 5.9 copy-start.56
  879.3 23.6 %all-to-all-start.4 = ((bf16[2,256,1536]{2,1,0:T(8,128)(2,1)}), bf16[2,256,1536]{2,1,0:T(8,128)(2,1)}, u32[]{:S(2)}, u32[]{:S(2)}) async-start(bf16[2,256,1536]{2,1,0:T(8,128)(2,1)} %broadcast_in_dim.51), calls=%async_computation.4 | async-start | bytes 3145728 | tf_op jit(solution)/shard_map/all_to_all | solution.py:37
  885.4 21.2 %copy-start.49 = (f32[1024]{0:T(1024)}, f32[1024]{0:T(1024)S(1)}, u32[]{:S(2)}) copy-start(f32[1024]{0:T(1024)S(1)} %reduce_sum.216) | copy-start | bytes 12292
  885.9 53.9 %copy-start.48 = (f32[256]{0:T(256)S(1)}, f32[256]{0:T(256)}, u32[]{:S(2)}) copy-start(f32[256]{0:T(256)} %copy-done.47) | copy-start | bytes 3076
  885.9 53.9 %copy-start.6 = (f32[256,1536]{1,0:T(8,128)S(1)}, f32[256,1536]{1,0:T(8,128)}, u32[]{:S(2)}) copy-start(f32[256,1536]{1,0:T(8,128)} %copy-done.4) | copy-start | bytes 4718596
  904.8 1.1 copy-start.7
  964.4 6.1 copy-start.29
  967.9 3.9 copy-start.28
  (6 other events, 5.8 us)
Sparse Core Ops, SparseCore 0:
  13.7 177.2 all-gather.2
  194.0 103.8 all-gather.4
  498.7 144.1 reduce-scatter.6
  647.3 221.0 reduce-scatter.4
  873.5 75.2 all-reduce.8
where the time goes:
time: 992 us; the launch traced here: 981 us
  waiting for transfers between devices  556 us (56%)
  matrix products  135 us (14%)
  local copies, waits for them, and re-layouts  129 us (13%)
  blocking collectives  63.9 us (6%)
  other arithmetic  52.3 us (5%)
  starting transfers between devices  28.6 us (3%)
  between operations  15.8 us (2%)
    all_gather x2, waiting for transfers between devices, turned_gather(): result, at, outs = (lax.all_gather(both, axis, axis=0, tiled=True), 0, [])  248 us
    reduce_scatter x1, waiting for transfers between devices, in_one_piece_2(): result = lax.psum_scatter(both, axis, scatter_dimension=dim, tiled=True)  221 us
    all_to_all x5, waiting for transfers between devices, from_everyone(): lax.all_to_all(jnp.broadcast_to(x[None], (size, *x.shape)), axis, 0, 0, t...  67 us
    concatenate x1, local copies, waits for them, and re-layouts, in_one_piece_2(): jnp.concatenate([a.reshape(*a.shape[:along], w) for a, w in zip(arrays, w...  56.5 us
    dot_general x7, matrix products, tail_dot(): lax.dot_general(left, right, (((1,), (1,)), ((), ())), preferred_element_...  42.8 us
    unnamed x125, local copies, waits for them, and re-layouts  36.5 us
    dot_general x7, matrix products, lead_dot(): lax.dot_general(left, right, (((0,), (0,)), ((), ())), preferred_element_...  35.2 us
    unnamed x1, blocking collectives  33.2 us
  transfers between devices with their start and end apart: 11, of which 8 were waited for; matrix products, arithmetic and copies ran while one was open for 20% of the time, Pallas kernels for 0%

commit v1 on v0

v1 whole, which is shorter than its diff:
```python
import jax
import jax.numpy as jnp
from jax import lax
from jax.experimental import pallas as pl
from jax.sharding import PartitionSpec as P

HD = 128


ROPE_BASE = 1000000.0
EPSILON = 1e-06


def rms_norm(values, gain_vec):
    return (
        values * lax.rsqrt(jnp.mean(values * values, axis=-1, keepdims=True) + EPSILON) * gain_vec
    )


def rope_tables(positions, head_width):
    half_width = head_width // 2
    freq_index = jnp.arange(half_width).astype(jnp.float32)
    inverse = ROPE_BASE ** (-(freq_index * 2.0 / head_width))
    angles = positions.astype(jnp.float32)[:, None] * inverse[None, :]
    cosine = jnp.cos(angles)
    sine_table = jnp.sin(angles)
    return (jnp.concatenate([cosine, cosine], -1), jnp.concatenate([sine_table, sine_table], -1))


def rotate(values, cosine, sine_table):
    half_width = values.shape[-1] // 2
    turned = jnp.concatenate([-values[..., half_width:], values[..., :half_width]], -1)
    return values * cosine[:, None, :] + turned * sine_table[:, None, :]


def segment_info(seq_lengths, total_rows):
    ends_at = jnp.cumsum(seq_lengths)
    places = jnp.arange(total_rows, dtype=jnp.int32)
    passed = places[:, None] >= ends_at[None, :]
    segment = jnp.sum(passed.astype(jnp.int32), axis=1)
    starts = jnp.sum(jnp.where(passed, seq_lengths[None, :], 0), axis=1)
    return (segment, places - starts)


def lead_dot(left, right):
    return lax.dot_general(
        left, right, (((0,), (0,)), ((), ())), preferred_element_type=jnp.float32
    )


def tail_dot(left, right):
    return lax.dot_general(
        left, right, (((1,), (1,)), ((), ())), preferred_element_type=jnp.float32
    )


def swap_sum(x, axis):
    low = x.astype(jnp.bfloat16)
    other = lax.ppermute(low, axis, [(0, 1), (1, 0)])
    return low.astype(jnp.float32) + other.astype(jnp.float32)


def hidden_range(width, parts, rank):
    tiles = width // 128
    span = -(-tiles // parts) * 128
    start = jnp.minimum(rank * span, width - span)
    return span, pl.multiple_of(start, 128), parts * span - width


def on_device(
    tokens,
    cotangent,
    lengths,
    gain_attn,
    w_query,
    b_query,
    w_key,
    b_key,
    w_value,
    b_value,
    w_out,
    gain_mlp,
    w_gate,
    w_up,
    w_down,
):
    bf16, f32 = jnp.bfloat16, jnp.float32
    row_count, width = tokens.shape
    context_size = lax.axis_size("context")
    context_rank = lax.axis_index("context")
    fsdp_rank = lax.axis_index("fsdp")
    shard = w_query.shape[0]
    query_cols, kv_cols, hidden_cols = w_query.shape[1], w_key.shape[1], w_gate.shape[1]
    heads_kv = kv_cols // HD
    heads_query = query_cols // HD
    per_group = heads_query // heads_kv
    score_scale = HD ** (-0.5)
    group_rows = row_count * context_size
    segment_all, position_all = segment_info(lengths[0], group_rows)
    first_row = context_rank * row_count
    segment_mine = lax.dynamic_slice_in_dim(segment_all, first_row, row_count)
    position_mine = lax.dynamic_slice_in_dim(position_all, first_row, row_count)
    query_at = first_row + jnp.arange(row_count, dtype=jnp.int32)
    key_at = jnp.arange(group_rows, dtype=jnp.int32)
    allowed = (segment_mine[:, None] == segment_all[None, :]) & (
        key_at[None, :] <= query_at[:, None]
    )
    cosine, sine_table = rope_tables(position_mine, HD)

    span, start, overlap = hidden_range(hidden_cols, context_size, context_rank)
    gains = jnp.pad(jnp.stack([gain_attn, gain_mlp], axis=1), ((0, 0), (0, 126)))
    attn_pack = jnp.concatenate([w_query, w_key, w_value, w_out.T, gains], axis=1)
    mlp_pack = jnp.concatenate(
        [lax.dynamic_slice_in_dim(w, start, span, axis=1) for w in (w_gate, w_up, w_down.T)], axis=1
    )
    attn_full = lax.all_gather(attn_pack, "fsdp", axis=0, tiled=True)
    mlp_full = lax.all_gather(mlp_pack, "fsdp", axis=0, tiled=True)
    lin_cols = query_cols + 2 * kv_cols
    lin_full = attn_full[:, :lin_cols]
    out_turned = attn_full[:, lin_cols : lin_cols + query_cols]
    gain_one = attn_full[:, lin_cols + query_cols].astype(f32)
    gain_two = attn_full[:, lin_cols + query_cols + 1].astype(f32)
    gate_full, lift_full, down_turned = (mlp_full[:, k * span : (k + 1) * span] for k in range(3))
    keep = (
        jnp.arange(span) >= jnp.where(context_rank == context_size - 1, overlap, 0)
    )[None, :]
    dy_group = lax.all_gather(cotangent, "context", axis=0, tiled=True)

    inputs = tokens.astype(f32)
    normed_one = rms_norm(inputs, gain_one).astype(bf16)
    bias = jnp.concatenate([b_query, b_key, b_value]).astype(f32)
    lin = jnp.dot(normed_one, lin_full, preferred_element_type=f32) + bias
    query_lin = lin[:, :query_cols]
    key_lin = lin[:, query_cols : query_cols + kv_cols]
    value_lin = lin[:, query_cols + kv_cols :]
    query_heads = rotate(query_lin.reshape(row_count, heads_query, HD), cosine, sine_table).astype(bf16)
    query_heads = query_heads.reshape(row_count, heads_kv, per_group, HD)
    key_heads = rotate(key_lin.reshape(row_count, heads_kv, HD), cosine, sine_table).astype(bf16)
    value_heads = value_lin.astype(bf16).reshape(row_count, heads_kv, HD)
    kv_group = lax.all_gather(
        jnp.concatenate([key_heads, value_heads], axis=1), "context", axis=0, tiled=True
    )
    key_group, value_group = kv_group[:, :heads_kv], kv_group[:, heads_kv:]
    scores = (
        jnp.einsum("qgjd,kgd->gjqk", query_heads, key_group, preferred_element_type=f32)
        * score_scale
    )
    scores = jnp.where(allowed, scores, -1e30)
    row_top = jnp.max(scores, axis=-1, keepdims=True)
    expo = jnp.exp(scores - row_top)
    probs = expo / jnp.sum(expo, axis=-1, keepdims=True)
    probs_low = probs.astype(bf16)
    mixed = jnp.einsum("gjqk,kgd->qgjd", probs_low, value_group, preferred_element_type=f32)
    mixed = mixed.reshape(row_count, heads_query * HD).astype(bf16)
    middle = inputs + swap_sum(tail_dot(mixed, out_turned), "tensor")
    normed_two = rms_norm(middle, gain_two).astype(bf16)

    normed_group = lax.all_gather(normed_two, "context", axis=0, tiled=True)
    d_hidden = jnp.dot(dy_group, down_turned, preferred_element_type=f32)
    gate_lin = jnp.dot(normed_group, gate_full, preferred_element_type=f32)
    lift_lin = jnp.dot(normed_group, lift_full, preferred_element_type=f32)
    sigmoid_gate = jax.nn.sigmoid(gate_lin)
    swish = gate_lin * sigmoid_gate
    hidden = jnp.where(keep, swish * lift_lin, 0.0).astype(bf16)
    d_gate = jnp.where(
        keep, d_hidden * lift_lin * sigmoid_gate * (1.0 + gate_lin * (1.0 - sigmoid_gate)), 0.0
    ).astype(bf16)
    d_lift = jnp.where(keep, d_hidden * swish, 0.0).astype(bf16)
    d_normed_part = tail_dot(d_gate, gate_full) + tail_dot(d_lift, lift_full)
    d_normed_two = swap_sum(
        lax.psum_scatter(d_normed_part.astype(bf16), "context", scatter_dimension=0, tiled=True),
        "tensor",
    )
    mlp_part = tail_dot(hidden, down_turned)
    mlp_branch = swap_sum(
        lax.psum_scatter(mlp_part.astype(bf16), "context", scatter_dimension=0, tiled=True),
        "tensor",
    )
    result = (middle + mlp_branch).astype(bf16)
    mlp_grads = jnp.concatenate(
        [
            lead_dot(normed_group, d_gate).astype(bf16),
            lead_dot(normed_group, d_lift).astype(bf16),
            lead_dot(dy_group, hidden).astype(bf16),
        ],
        axis=1,
    )
    mlp_shard = lax.psum_scatter(mlp_grads, "fsdp", scatter_dimension=0, tiled=True)
    mlp_all = lax.all_gather(mlp_shard, "context", axis=0)

    def whole(k):
        parts = [mlp_all[i, :, k * span : (k + 1) * span] for i in range(context_size)]
        parts[-1] = parts[-1][:, overlap:]
        return jnp.concatenate(parts, axis=1).astype(f32)

    _, pull_two = jax.vjp(rms_norm, middle, gain_two)
    d_middle_norm, grad_gain_mlp = pull_two(d_normed_two)
    d_middle = cotangent.astype(f32) + d_middle_norm
    d_branch = d_middle.astype(bf16)
    grad_w_out = lead_dot(d_branch, mixed)
    d_mixed = (
        jnp.dot(d_branch, out_turned, preferred_element_type=f32)
        .astype(bf16)
        .reshape(row_count, heads_kv, per_group, HD)
    )
    d_probs = jnp.einsum("qgjd,kgd->gjqk", d_mixed, value_group, preferred_element_type=f32)
    inner = jnp.sum(probs * d_probs, axis=-1, keepdims=True)
    d_scores = (probs * (d_probs - inner)).astype(bf16)
    d_query = (
        jnp.einsum("gjqk,kgd->qgjd", d_scores, key_group, preferred_element_type=f32) * score_scale
    )
    d_key_part = (
        jnp.einsum("gjqk,qgjd->kgd", d_scores, query_heads, preferred_element_type=f32)
        * score_scale
    )
    d_value_part = jnp.einsum("gjqk,qgjd->kgd", probs_low, d_mixed, preferred_element_type=f32)
    d_kv = lax.psum_scatter(
        jnp.concatenate([d_key_part, d_value_part], axis=1), "context", scatter_dimension=0, tiled=True
    )
    d_key, d_value = d_kv[:, :heads_kv], d_kv[:, heads_kv:]

    def turn_query(values):
        return rotate(values, cosine, sine_table)

    _, pull_query = jax.vjp(turn_query, query_lin.reshape(row_count, heads_query, HD))
    _, pull_key = jax.vjp(turn_query, key_lin.reshape(row_count, heads_kv, HD))
    d_query_lin = pull_query(d_query.reshape(row_count, heads_query, HD))[0]
    d_key_lin = pull_key(d_key)[0]
    d_lin = jnp.concatenate(
        [
            d_query_lin.reshape(row_count, query_cols),
            d_key_lin.reshape(row_count, kv_cols),
            d_value.reshape(row_count, kv_cols),
        ],
        axis=1,
    ).astype(bf16)
    bias_part = jnp.sum(d_lin.astype(f32), axis=0)
    attn_grads = jnp.concatenate(
        [lead_dot(normed_one, d_lin).astype(bf16), grad_w_out.astype(bf16)], axis=1
    )
    attn_shard = lax.psum(
        lax.psum_scatter(attn_grads, "fsdp", scatter_dimension=0, tiled=True), "context"
    ).astype(f32)
    d_normed_one = swap_sum(tail_dot(d_lin, lin_full), "tensor")
    _, pull_one = jax.vjp(rms_norm, inputs, gain_one)
    d_input_norm, grad_gain_attn = pull_one(d_normed_one)
    grad_tokens = d_middle + d_input_norm
    small = lax.psum(
        jnp.concatenate([grad_gain_attn, grad_gain_mlp, bias_part]), ("fsdp", "context")
    )
    own = lambda at: lax.dynamic_slice_in_dim(small, at + fsdp_rank * shard, shard)
    bias_total = small[2 * width :]
    return (
        result,
        grad_tokens,
        own(0),
        attn_shard[:, :query_cols],
        bias_total[:query_cols],
        attn_shard[:, query_cols : query_cols + kv_cols],
        bias_total[query_cols : query_cols + kv_cols],
        attn_shard[:, query_cols + kv_cols : lin_cols],
        bias_total[query_cols + kv_cols :],
        attn_shard[:, lin_cols:].T,
        own(width),
        whole(0),
        whole(1),
        whole(2).T,
    )


def solution(mesh):
    return jax.shard_map(
        on_device,
        mesh=mesh,
        in_specs=(
            P(("fsdp", "context"), None),
            P(("fsdp", "context"), None),
            P("fsdp", None),
            P("fsdp"),
            P("fsdp", "tensor"),
            P("tensor"),
            P("fsdp", "tensor"),
            P("tensor"),
            P("fsdp", "tensor"),
            P("tensor"),
            P("tensor", "fsdp"),
            P("fsdp"),
            P("fsdp", "tensor"),
            P("fsdp", "tensor"),
            P("tensor", "fsdp"),
        ),
        out_specs=(
            P(("fsdp", "context"), None),
            P(("fsdp", "context"), None),
            P("fsdp"),
            P("fsdp", "tensor"),
            P("tensor"),
            P("fsdp", "tensor"),
            P("tensor"),
            P("fsdp", "tensor"),
            P("tensor"),
            P("tensor", "fsdp"),
            P("fsdp"),
            P("fsdp", "tensor"),
            P("fsdp", "tensor"),
            P("tensor", "fsdp"),
        ),
        check_vma=False,
    )
```

time: 992 us -> 1020 us (1.028)
  blocking collectives: 63.9 us -> 341 us
  waiting for transfers between devices: 556 us -> 440 us
  local copies, waits for them, and re-layouts: 129 us -> 53.9 us
  matrix products: 135 us -> 93.3 us
  starting transfers between devices: 28.6 us -> 15.7 us
    psum x1, blocking collectives: 17.5 us -> 325 us  [on_device(): lax.psum(jnp.concatenate([grad_gain_attn, grad_gain_mlp, bias_part]), ('f...]
    all_gather x2 -> x5, waiting for transfers between devices: 248 us -> 160 us  [the longest x1 69.2 us: on_device(): mlp_full = lax.all_gather(mlp_pack, 'fsdp', axis=0, tiled=True)]
    all_to_all x6 -> x0, waiting for transfers between devices: 73.3 us -> none  [the longest x5 67 us: from_everyone(): lax.all_to_all(jnp.broadcast_to(x[None], (size, *x.shape)), axis, 0, 0, t...]
    concatenate x2 -> x3, local copies, waits for them, and re-layouts: 61.3 us -> 0.87 us  [the longest x1 0.76 us: rope_tables(): jnp.concatenate([cosine, cosine], -1)]
    ppermute x0 -> x4, waiting for transfers between devices: none -> 51 us  [swap_sum(): other = lax.ppermute(low, axis, [(0, 1), (1, 0)])]
    unnamed x1 -> x0, blocking collectives: 33.2 us -> none
    reduce_scatter x1 -> x4, waiting for transfers between devices: 221 us -> 190 us  [the longest x1 114 us: on_device(): lax.psum_scatter(mlp_grads, 'fsdp', scatter_dimension=0, tiled=True)]
    all_to_all x6 -> x0, starting transfers between devices: 28 us -> none  [the longest x5 23.7 us: from_everyone(): lax.all_to_all(jnp.broadcast_to(x[None], (size, *x.shape)), axis, 0, 0, t...]
  transfers between devices with their start and end apart: 11 -> 15, of which waited for: 8 -> 11; matrix products, arithmetic and copies ran while one was open for 20% -> 12% of each run, Pallas kernels for 0% -> 0%
where the time goes in v1:
time: 1020 us; the launch traced here: 1010 us
  waiting for transfers between devices  440 us (43%)
  blocking collectives  341 us (33%)
  matrix products  93.3 us (9%)
  local copies, waits for them, and re-layouts  53.9 us (5%)
  other arithmetic  52.8 us (5%)
  starting transfers between devices  15.7 us (2%)
  between operations  15.2 us (1%)
    psum x1, blocking collectives, on_device(): lax.psum(jnp.concatenate([grad_gain_attn, grad_gain_mlp, bias_part]), ('f...  325 us
    reduce_scatter x1, waiting for transfers between devices, on_device(): lax.psum_scatter(mlp_grads, 'fsdp', scatter_dimension=0, tiled=True)  114 us
    all_gather x1, waiting for transfers between devices, on_device(): mlp_full = lax.all_gather(mlp_pack, 'fsdp', axis=0, tiled=True)  69.2 us
    all_gather x1, waiting for transfers between devices, on_device(): attn_full = lax.all_gather(attn_pack, 'fsdp', axis=0, tiled=True)  60.4 us
    ppermute x4, waiting for transfers between devices, swap_sum(): other = lax.ppermute(low, axis, [(0, 1), (1, 0)])  51 us
    unnamed x12, waiting for transfers between devices  39 us
    reduce_scatter x1, waiting for transfers between devices, on_device(): lax.psum_scatter(mlp_part.astype(bf16), 'context', scatter_dimension=0, t...  38.8 us
    unnamed x108, local copies, waits for them, and re-layouts  36.1 us
  transfers between devices with their start and end apart: 15, of which 11 were waited for; matrix products, arithmetic and copies ran while one was open for 12% of the time, Pallas kernels for 0%

profile of v1, /device:TPU:0, one launch (start us, length us, event | category | flops | bytes accessed | tf_op | source)
XLA Modules:
  0.0 1011.7 jit_solution(15932514782396755356)
XLA Ops:
  13.3 1.3 constant_dynamic-slice_fusion
  17.1 60.4 %all-gather.7.cloned.1.call-done = bf16[1536,1920]{1,0:T(8,128)(2,1)} async-done(((bf16[96,1920]{1,0:T(8,128)(2,1)}), bf16[1536,1920]{1,0:T(8,128)(2,1)}) %all-gather.7.cloned.1.call-update) | async-done | bytes 5898256 | tf_op jit(solution)/shard_map/all_gather | solution.py:116
  77.5 1.7 convert_reduce_fusion.1
  79.3 2.9 fusion.50
  83.2 1.4 copy.122
  85.9 1.1 copy.124
  88.8 1.1 copy.121
  90.0 1.7 add_convert_fusion.4
  92.8 15.7 %all_gather.22 = bf16[1024,2,128]{2,0,1:T(8,128)(2,1)S(1)} all-gather(bf16[256,2,128]{2,0,1:T(8,128)(2,1)S(1)} %pad_maximum_fusion.7), channel_id=1, replica_groups=mesh['fsdp'=16,'context'=4,'tensor'=2] {'context'}, dimensions={0}, use_global_device_ids=true | all-gather | bytes 655360 | tf_op jit(solution)/shard_map/all_gather | solution.py:140
  108.5 1.1 fusion.6
  109.7 1.3 fusion.5
  111.0 1.3 copy-done.2
  112.3 1.9 fusion.57
  114.2 2.6 convolution_convert_fusion.6
  117.5 17.8 %collective-permute-done = bf16[256,1536]{1,0:T(8,128)(2,1)S(1)} collective-permute-done((bf16[256,1536]{1,0:T(8,128)(2,1)S(1)}, bf16[256,1536]{1,0:T(8,128)(2,1)S(1)}, u32[]{:S(2)}, u32[]{:S(2)}) %collective-permute-start) | collective-permute-done | bytes 786464 | tf_op jit(solution)/shard_map/ppermute | solution.py:59
  135.9 1.1 multiply_convert_fusion
  137.3 69.2 %all-gather.11.cloned.1.call-done = bf16[1536,3456]{1,0:T(8,128)(2,1)} async-done(((bf16[96,3456]{1,0:T(8,128)(2,1)}), bf16[1536,3456]{1,0:T(8,128)(2,1)}) %all-gather.11.cloned.1.call-update) | async-done | bytes 10616848 | tf_op jit(solution)/shard_map/all_gather | solution.py:117
  206.6 9.3 fusion.19
  215.8 30.1 %all-gather.9.cloned.1.call-done = bf16[1024,1536]{1,0:T(8,128)(2,1)} async-done(((bf16[256,1536]{1,0:T(8,128)(2,1)}), bf16[1024,1536]{1,0:T(8,128)(2,1)}) %all-gather.9.cloned.1.call-update) | async-done | bytes 3145744 | tf_op jit(solution)/shard_map/all_gather | solution.py:158
  245.9 9.5 fusion.23
  255.4 9.9 fusion.12
  265.4 6.1 fusion.25
  271.4 5.8 add_convert_fusion
  277.3 10.4 %reduce-scatter.10.cloned.1.call-start = ((), (), s32[]{:S(2)}) async-start(), calls=%async_computation.8 | async-start | bytes 3932160 | tf_op jit(solution)/shard_map/reduce_scatter | solution.py:176
  287.7 8.6 convolution_convert_fusion.4
  296.4 19.4 %reduce-scatter.12.cloned.1.call-done = bf16[256,1536]{1,0:T(8,128)(2,1)} async-done(((bf16[1024,1536]{1,0:T(8,128)(2,1)}), bf16[256,1536]{1,0:T(8,128)(2,1)}) %reduce-scatter.12.cloned.1.call-update) | async-done | bytes 786448 | tf_op jit(solution)/shard_map/reduce_scatter | solution.py:171
  315.9 1.5 collective-permute-start.2
  317.3 38.8 %reduce-scatter.10.cloned.1.call-done = bf16[256,1536]{1,0:T(8,128)(2,1)} async-done(((bf16[1024,1536]{1,0:T(8,128)(2,1)}), bf16[256,1536]{1,0:T(8,128)(2,1)}) %reduce-scatter.10.cloned.1.call-update) | async-done | bytes 786448 | tf_op jit(solution)/shard_map/reduce_scatter | solution.py:176
  356.1 1.5 collective-permute-start.1
  357.6 2.0 multiply_reduce_fusion
  359.6 16.1 %collective-permute-done.1 = bf16[256,1536]{1,0:T(8,128)(2,1)S(1)} collective-permute-done((bf16[256,1536]{1,0:T(8,128)(2,1)}, bf16[256,1536]{1,0:T(8,128)(2,1)S(1)}, u32[]{:S(2)}, u32[]{:S(2)}) %collective-permute-start.1) | collective-permute-done | bytes 786464 | tf_op jit(solution)/shard_map/ppermute | solution.py:59
  375.7 2.9 fusion.44
  378.6 1.1 copy-done.4
  379.7 3.4 fusion.54
  383.1 1.9 copy.130
  385.0 4.7 fusion.60
  389.8 2.1 fusion.1
  392.0 2.0 fusion.14
  393.9 1.7 copy-done.3
  397.8 2.6 broadcast_multiply_fusion
  400.7 2.2 convolution_convert_fusion.5
  403.0 18.1 %reduce-scatter.14.cloned.1.call-done = f32[256,2,128]{2,0,1:T(8,128)} async-done(((f32[1024,2,128]{2,0,1:T(8,128)}), f32[256,2,128]{2,0,1:T(8,128)}) %reduce-scatter.14.cloned.1.call-update) | async-done | bytes 262160 | tf_op jit(solution)/shard_map/reduce_scatter | solution.py:217
  424.4 1.1 convolution_convert_fusion.3
  426.1 2.8 pad_maximum_fusion.1
  428.9 8.1 copy.160
  437.3 6.6 fusion
  444.0 4.3 convolution_convert_fusion.1
  448.2 4.3 convolution_convert_fusion.2
  452.5 18.5 %pad_maximum_fusion = bf16[1536,3456]{0,1:T(8,128)(2,1)} fusion(bf16[1536,1152]{0,1:T(8,128)(2,1)S(1)} %fusion, bf16[1536,1152]{0,1:T(8,128)(2,1)S(1)} %convolution_convert_fusion.1, bf16[1536,1152]{0,1:T(8,128)(2,1)S(1)} %convolution_convert_fusion.2), kind=kLoop, calls=%fused_computation | loop fusion | flops 31850496 | bytes 21233664 | tf_op jit(solution)/shard_map/concatenate | solution.py:180
  471.0 13.7 %copy.162 = bf16[1536,3456]{1,0:T(8,128)(2,1)} copy(bf16[1536,3456]{0,1:T(8,128)(2,1)} %pad_maximum_fusion) | data formatting | bytes 21233664
  484.8 38.1 %reduce-scatter.16.cloned.1.call-done = bf16[96,1792]{1,0:T(8,128)(2,1)} async-done(((bf16[1536,1792]{1,0:T(8,128)(2,1)}), bf16[96,1792]{1,0:T(8,128)(2,1)}) %reduce-scatter.16.cloned.1.call-update) | async-done | bytes 344080
  523.0 2.0 copy.161
  525.2 113.9 %reduce-scatter.18.cloned.1.call-done = bf16[96,3456]{1,0:T(8,128)(2,1)} async-done(((bf16[1536,3456]{1,0:T(8,128)(2,1)}), bf16[96,3456]{1,0:T(8,128)(2,1)}) %reduce-scatter.18.cloned.1.call-update) | async-done | bytes 663568 | tf_op jit(solution)/shard_map/reduce_scatter | solution.py:188
  639.2 3.1 fusion.33
  642.9 1.2 convert_reduce_fusion
  644.1 17.0 %collective-permute-done.3 = bf16[256,1536]{1,0:T(8,128)(2,1)} collective-permute-done((bf16[256,1536]{1,0:T(8,128)(2,1)S(1)}, bf16[256,1536]{1,0:T(8,128)(2,1)}, u32[]{:S(2)}, u32[]{:S(2)}) %collective-permute-start.3) | collective-permute-done | bytes 786464 | tf_op jit(solution)/shard_map/ppermute | solution.py:59
  661.2 1.8 fusion.43
  663.0 325.0 %psum.14 = f32[4096]{0:T(1024)S(1)} all-reduce(f32[4096]{0:T(1024)S(1)} %pad_maximum_fusion.8), channel_id=1, replica_groups=mesh['fsdp'=16,'context'=4,'tensor'=2] {'fsdp','context'}, use_global_device_ids=true, to_apply=%region_16.17 | all-reduce | flops 4096 | bytes 32768 | tf_op jit(solution)/shard_map/psum | solution.py:248
  989.7 2.9 fusion.45
  996.6 1.1 convert_element_type.220
  998.6 2.1 slice_bitcast_fusion.10
  1000.8 1.3 maximum_convert_fusion
  1002.1 1.3 maximum_convert_fusion.1
  1003.4 1.3 convert_bitcast_fusion
  (183 shorter events, 29.3 us)
Async XLA Ops:
  7.2 6.0 copy-start
  7.2 8.3 copy-start.38
  7.2 8.8 copy-start.36
  7.2 8.8 copy-start.37
  7.2 8.8 copy-start.35
  7.2 8.8 copy-start.6
  7.2 70.3 %all-gather.7.cloned.1.call-start = ((), (), s32[]{:S(2)}) async-start(), calls=%async_computation.5 | async-start | bytes 6266880 | tf_op jit(solution)/shard_map/all_gather | solution.py:116
  11.6 0.7 copy-start.26
  12.3 125.0 %all-gather.13.cloned.1.call-start = ((), (), s32[]{:S(2)}) async-start(), calls=%async_computation.9 | async-start | bytes 3932160 | tf_op jit(solution)/shard_map/all_gather | solution.py:127
  13.1 193.5 %all-gather.11.cloned.1.call-start = ((), (), s32[]{:S(2)}) async-start(), calls=%async_computation.7 | async-start | bytes 11280384 | tf_op jit(solution)/shard_map/all_gather | solution.py:117
  15.5 230.4 %all-gather.9.cloned.1.call-start = ((), (), s32[]{:S(2)}) async-start(), calls=%async_computation.6 | async-start | bytes 3932160 | tf_op jit(solution)/shard_map/all_gather | solution.py:158
  16.3 65.9 %copy-start.33 = (f32[256]{0:T(256)}, f32[256]{0:T(256)S(1)}, u32[]{:S(2)}) copy-start(f32[256]{0:T(256)S(1)} %fusion.46) | copy-start | bytes 3076
  16.3 65.9 %copy-start.31 = (f32[256]{0:T(256)}, f32[256]{0:T(256)S(1)}, u32[]{:S(2)}) copy-start(f32[256]{0:T(256)S(1)} %fusion.83) | copy-start | bytes 3076
  16.8 68.0 %copy-start.19 = (f32[256,64]{1,0:T(8,128)}, f32[256,64]{1,0:T(8,128)S(1)}, u32[]{:S(2)}) copy-start(f32[256,64]{1,0:T(8,128)S(1)} %get-tuple-element.115) | copy-start | bytes 196612
  16.8 68.0 %copy-start.21 = (f32[256,64]{1,0:T(8,128)}, f32[256,64]{1,0:T(8,128)S(1)}, u32[]{:S(2)}) copy-start(f32[256,64]{1,0:T(8,128)S(1)} %get-tuple-element.114) | copy-start | bytes 196612
  82.2 3.6 copy-start.11
  85.7 1.3 copy-start.23
  85.8 1.3 copy-start.27
  85.9 5.8 copy-start.9
  108.5 2.4 copy-start.14
  109.7 2.6 copy-start.2
  114.2 21.6 %copy-start.28 = (bf16[128,6,256]{2,0,1:T(8,128)(2,1)}, bf16[128,6,256]{2,0,1:T(8,128)(2,1)S(1)}, u32[]{:S(2)}) copy-start(bf16[128,6,256]{2,0,1:T(8,128)(2,1)S(1)} %fusion.57) | copy-start | bytes 1179652
  116.9 18.5 %collective-permute-start = (bf16[256,1536]{1,0:T(8,128)(2,1)S(1)}, bf16[256,1536]{1,0:T(8,128)(2,1)S(1)}, u32[]{:S(2)}, u32[]{:S(2)}) collective-permute-start(bf16[256,1536]{1,0:T(8,128)(2,1)S(1)} %convolution_convert_fusion.6), channel_id=1, source_target_pairs={{0,1},{1,0},{2,3},{3,2},{4,5},{5,4},{6,7},{7,6},{8,9},{9,8},{10,11... | collective-permute-start | bytes 2359304 | tf_op jit(solution)/shard_map/ppermute | solution.py:59
  137.0 178.9 %reduce-scatter.12.cloned.1.call-start = ((), (), s32[]{:S(2)}) async-start(), calls=%async_computation.10 | async-start | bytes 3932160 | tf_op jit(solution)/shard_map/reduce_scatter | solution.py:171
  245.9 9.5 copy-start.39
  245.9 9.5 copy-start.40
  245.9 9.5 copy-start.42
  265.4 6.1 copy-start.44
  277.3 78.8 %reduce-scatter.10.cloned.1.call-start = ((), (), s32[]{:S(2)}) async-start(), calls=%async_computation.8 | async-start | bytes 3932160 | tf_op jit(solution)/shard_map/reduce_scatter | solution.py:176
  296.4 79.3 %copy-start.12 = (bf16[256,1536]{1,0:T(8,128)(2,1)S(1)}, bf16[256,1536]{1,0:T(8,128)(2,1)}, u32[]{:S(2)}) copy-start(bf16[256,1536]{1,0:T(8,128)(2,1)} %param.16) | copy-start | bytes 2359300
  296.4 124.7 %reduce-scatter.14.cloned.1.call-start = ((), (), s32[]{:S(2)}) async-start(), calls=%async_computation.11 | async-start | bytes 1310720 | tf_op jit(solution)/shard_map/reduce_scatter | solution.py:217
  315.9 41.7 %collective-permute-start.2 = (bf16[256,1536]{1,0:T(8,128)(2,1)}, bf16[256,1536]{1,0:T(8,128)(2,1)}, u32[]{:S(2)}, u32[]{:S(2)}) collective-permute-start(bf16[256,1536]{1,0:T(8,128)(2,1)} %reduce-scatter.12.cloned.1.call-done), channel_id=1, source_target_pairs={{0,1},{1,0},{2,3},{3,2},{4,5},{5,4},{6,7},{7,6},{8,9},{9,8},{10,11... | collective-permute-start | bytes 2359304 | tf_op jit(solution)/shard_map/ppermute | solution.py:59
  356.1 19.6 %copy-start.13 = (bf16[256,1536]{1,0:T(8,128)(2,1)S(1)}, bf16[256,1536]{1,0:T(8,128)(2,1)}, u32[]{:S(2)}) copy-start(bf16[256,1536]{1,0:T(8,128)(2,1)} %reduce-scatter.12.cloned.1.call-done) | copy-start | bytes 2359300
  356.1 19.6 %copy-start.25 = (bf16[256,1536]{1,0:T(8,128)(2,1)S(1)}, bf16[256,1536]{1,0:T(8,128)(2,1)}, u32[]{:S(2)}) copy-start(bf16[256,1536]{1,0:T(8,128)(2,1)} %reduce-scatter.10.cloned.1.call-done) | copy-start | bytes 2359300
  356.1 19.5 %collective-permute-start.1 = (bf16[256,1536]{1,0:T(8,128)(2,1)}, bf16[256,1536]{1,0:T(8,128)(2,1)S(1)}, u32[]{:S(2)}, u32[]{:S(2)}) collective-permute-start(bf16[256,1536]{1,0:T(8,128)(2,1)} %reduce-scatter.10.cloned.1.call-done), channel_id=1, source_target_pairs={{0,1},{1,0},{2,3},{3,2},{4,5},{5,4},{6,7},{7,6},{8,9},{9,8},{10,11... | collective-permute-start | bytes 2359304 | tf_op jit(solution)/shard_map/ppermute | solution.py:59
  378.6 1.1 copy-start.4
  379.7 10.0 slice-start
  385.0 4.8 slice-start.1
  385.0 4.8 copy-start.15
  385.0 4.8 copy-start.30
  391.9 3.7 copy-start.10
  391.9 3.7 copy-start.17
  393.9 1.7 copy-start.3
  395.6 2.2 copy-start.16
  395.6 2.2 copy-start.24
  397.7 3.0 copy-start.5
  397.7 125.2 %reduce-scatter.16.cloned.1.call-start = ((), (), s32[]{:S(2)}) async-start(), calls=%async_computation.14 | async-start | bytes 5849088
  397.8 2.9 copy-start.29
  400.5 21.6 %copy-start.20 = (f32[256,64]{1,0:T(8,128)S(1)}, f32[256,64]{1,0:T(8,128)}, u32[]{:S(2)}) copy-start(f32[256,64]{1,0:T(8,128)} %copy-done.19) | copy-start | bytes 196612
  400.7 24.9 %copy-start.18 = (bf16[256,6,128]{0,2,1:T(8,128)(2,1)}, bf16[256,6,128]{0,2,1:T(8,128)(2,1)S(1)}, u32[]{:S(2)}) copy-start(bf16[256,6,128]{0,2,1:T(8,128)(2,1)S(1)} %add_convert_fusion.3) | copy-start | bytes 1179652
  400.7 22.5 %copy-start.22 = (f32[256,64]{1,0:T(8,128)S(1)}, f32[256,64]{1,0:T(8,128)}, u32[]{:S(2)}) copy-start(f32[256,64]{1,0:T(8,128)} %copy-done.21) | copy-start | bytes 196612
  400.7 23.7 %copy-start.7 = (bf16[256,1536]{1,0:T(8,128)(2,1)S(1)}, bf16[256,1536]{1,0:T(8,128)(2,1)}, u32[]{:S(2)}) copy-start(bf16[256,1536]{1,0:T(8,128)(2,1)} %param.15) | copy-start | bytes 2359300
  400.7 23.7 %copy-start.32 = (f32[256]{0:T(256)S(1)}, f32[256]{0:T(256)}, u32[]{:S(2)}) copy-start(f32[256]{0:T(256)} %copy-done.31) | copy-start | bytes 3076
  424.4 1.7 copy-start.8
  437.0 202.2 %reduce-scatter.18.cloned.1.call-start = ((), (), s32[]{:S(2)}) async-start(), calls=%async_computation.15 | async-start | bytes 11280384 | tf_op jit(solution)/shard_map/reduce_scatter | solution.py:188
  437.3 6.6 copy-start.41
  437.3 6.6 copy-start.45
  443.9 4.3 copy-start.43
  484.8 507.8 %all-reduce.7.cloned.1.call-start = ((), (), s32[]{:S(2)}) async-start(), calls=%async_computation.12 | async-start | bytes 917504 | tf_op jit(solution)/shard_map/psum | solution.py:241
  524.9 473.7 %all-gather.15.cloned.1.call-start = ((), (), s32[]{:S(2)}) async-start(), calls=%async_computation.13 | async-start | bytes 3317760 | tf_op jit(solution)/shard_map/all_gather | solution.py:189
  639.2 350.0 %copy-start.34 = (f32[256]{0:T(256)S(1)}, f32[256]{0:T(256)}, u32[]{:S(2)}) copy-start(f32[256]{0:T(256)} %copy-done.33) | copy-start | bytes 3076
  642.3 18.9 %collective-permute-start.3 = (bf16[256,1536]{1,0:T(8,128)(2,1)S(1)}, bf16[256,1536]{1,0:T(8,128)(2,1)}, u32[]{:S(2)}, u32[]{:S(2)}) collective-permute-start(bf16[256,1536]{1,0:T(8,128)(2,1)S(1)} %fusion.33), channel_id=1, source_target_pairs={{0,1},{1,0},{2,3},{3,2},{4,5},{5,4},{6,7},{7,6},{8,9},{9,8},{10,11... | collective-permute-start | bytes 2359304 | tf_op jit(solution)/shard_map/ppermute | solution.py:59
  1000.8 3.9 copy-start.1
Sparse Core Ops, SparseCore 0:
  12.5 65.0 all-gather.6
  79.2 41.4 all-gather.12
  123.8 82.7 all-gather.10
  208.7 37.2 all-gather.8
  277.4 38.4 reduce-scatter.11
  318.1 37.9 reduce-scatter.9
  397.8 23.2 reduce-scatter.13
  437.1 85.7 reduce-scatter.15
  527.3 111.8 reduce-scatter.17
  642.0 41.0 all-reduce.6
  684.9 36.4 all-gather.14

commit v2 on v1

--- a/solution.py
+++ b/solution.py
@@ -2,13 +2,454 @@
 import jax.numpy as jnp
 from jax import lax
 from jax.experimental import pallas as pl
+from jax.experimental.pallas import tpu as pltpu
 from jax.sharding import PartitionSpec as P
 
 HD = 128
-
+MESH = pl.DeviceIdType.MESH
+ANY = pl.BlockSpec(memory_space=pl.ANY)
+VM = pl.BlockSpec(memory_space=pltpu.VMEM)
+f32, bf16 = jnp.float32, jnp.bfloat16
 
 ROPE_BASE = 1000000.0
 EPSILON = 1e-06
+
+def meet(targets):
+    barrier = pltpu.get_barrier_semaphore()
+    for t in targets:
+        pl.semaphore_signal(barrier, inc=1, device_id=t, device_id_type=MESH)
+    pl.semaphore_wait(barrier, len(targets))
+
+def gather_kernel(x_ref, y_ref, w_ref, g_ref, send, recv, local):
+    shard = x_ref.shape[0]
+    rows = y_ref.shape[0]
+    f = lax.axis_index("fsdp"); c = lax.axis_index("context")
+    n, m = lax.axis_size("fsdp"), lax.axis_size("context")
+    core = lambda i: i + 1 - 2 * lax.rem(i, 2)
+    far = lambda i: i + 2 - 4 * lax.rem(lax.div(i, 2), 2)
+    up = lambda i: lax.rem(i + 4, n)
+    down = lambda i: lax.rem(i + n - 4, n)
+    nxt, prv = lax.rem(c + 1, m), lax.rem(c + m - 1, m)
+    F = lambda i: {"fsdp": i}
+    C = lambda i: {"context": i}
+    meet([F(core(f)), F(far(f)), F(up(f)), F(down(f)), C(nxt), C(prv)])
+    own = pltpu.make_async_copy(x_ref, w_ref.at[pl.ds(f * shard, shard)], local.at[0])
+    own.start()
+    own2 = pltpu.make_async_copy(y_ref, g_ref.at[pl.ds(c * rows, rows)], local.at[1])
+    own2.start()
+    half = shard // 2
+    started = []
+    def push(k, ref, at, size, to, src=None):
+        win = ref.at[pl.ds(pl.multiple_of(at, 16), size)]
+        cp = pltpu.make_async_remote_copy(win if src is None else src, win, send.at[k], recv.at[k],
+                                          device_id=to, device_id_type=MESH)
+        cp.start(); started.append(cp)
+    def land(k, ref, at, size, like):
+        win = ref.at[pl.ds(pl.multiple_of(at, 16), size)]
+        pltpu.make_async_remote_copy(win, win, send.at[k], recv.at[k], device_id=like, device_id_type=MESH).wait_recv()
+    push(0, w_ref, f * shard, shard, F(far(f)), x_ref)
+    push(1, w_ref, f * shard, shard, F(up(f)), x_ref)
+    push(2, w_ref, f * shard, shard, F(down(f)), x_ref)
+    push(20, g_ref, c * rows, rows, C(nxt), y_ref)
+    push(21, g_ref, c * rows, rows, C(prv), y_ref)
+    push(3, w_ref, f * shard, shard, F(core(f)), x_ref)
+    p = far(f)
+    land(0, w_ref, p * shard, shard, F(p))
+    push(4, w_ref, p * shard, shard, F(up(f)))
+    push(5, w_ref, p * shard, shard, F(down(f)))
+    push(6, w_ref, p * shard, shard, F(core(f)))
+    a, b = down(f), up(f)
+    land(1, w_ref, a * shard, shard, F(a))
+    push(7, w_ref, a * shard, half, F(up(f)))
+    push(8, w_ref, a * shard, shard, F(core(f)))
+    land(2, w_ref, b * shard, shard, F(b))
+    push(9, w_ref, b * shard + half, half, F(down(f)))
+    push(10, w_ref, b * shard, shard, F(core(f)))
+    hr = rows // 2
+    land(20, g_ref, prv * rows, rows, C(prv))
+    push(22, g_ref, prv * rows, hr, C(nxt))
+    land(21, g_ref, nxt * rows, rows, C(nxt))
+    push(23, g_ref, nxt * rows + hr, hr, C(prv))
+    a2, b2 = far(a), far(b)
+    land(4, w_ref, a2 * shard, shard, F(a))
+    push(11, w_ref, a2 * shard, half, F(up(f)))
+    push(12, w_ref, a2 * shard, shard, F(core(f)))
+    land(5, w_ref, b2 * shard, shard, F(b))
+    push(13, w_ref, b2 * shard + half, half, F(down(f)))
+    push(14, w_ref, b2 * shard, shard, F(core(f)))
+    o = lax.rem(f + 8, n); o2 = far(o)
+    land(7, w_ref, o * shard, half, F(a))
+    push(15, w_ref, o * shard, half, F(core(f)))
+    land(9, w_ref, o * shard + half, half, F(b))
+    push(16, w_ref, o * shard + half, half, F(core(f)))
+    land(11, w_ref, o2 * shard, half, F(a))
+    push(17, w_ref, o2 * shard, half, F(core(f)))
+    land(13, w_ref, o2 * shard + half, half, F(b))
+    push(18, w_ref, o2 * shard + half, half, F(core(f)))
+    s = core(f)
+    sib = F(s)
+    land(3, w_ref, s * shard, shard, sib)
+    land(6, w_ref, far(s) * shard, shard, sib)
+    land(8, w_ref, down(s) * shard, shard, sib)
+    land(10, w_ref, up(s) * shard, shard, sib)
+    land(12, w_ref, far(down(s)) * shard, shard, sib)
+    land(14, w_ref, far(up(s)) * shard, shard, sib)
+    so = lax.rem(s + 8, n)
+    land(15, w_ref, so * shard, half, sib)
+    land(16, w_ref, so * shard + half, half, sib)
+    land(17, w_ref, far(so) * shard, half, sib)
+    land(18, w_ref, far(so) * shard + half, half, sib)
+    cf = lax.rem(c + 2, m)
+    land(22, g_ref, cf * rows, hr, C(prv))
+    land(23, g_ref, cf * rows + hr, hr, C(nxt))
+    for cp in started: cp.wait_send()
+    own.wait(); own2.wait()
+
+def gather(x, y, cid=1):
+    shard, cols = x.shape; rows, width = y.shape
+    return pl.pallas_call(gather_kernel,
+        out_shape=(jax.ShapeDtypeStruct((16*shard, cols), x.dtype), jax.ShapeDtypeStruct((4*rows, width), y.dtype)),
+        in_specs=[ANY]*2, out_specs=(ANY, ANY),
+        scratch_shapes=[pltpu.SemaphoreType.DMA((24,)), pltpu.SemaphoreType.DMA((24,)), pltpu.SemaphoreType.DMA((2,))],
+        compiler_params=pltpu.CompilerParams(collective_id=cid, has_side_effects=True), name="gather_rows")(x, y)
+
+def norm_kernel(part_ref, x_ref, gain_ref, mid_ref, out_ref, other, normed, send, recv, local):
+    rows = part_ref.shape[0]
+    chunks = 4
+    size = rows // chunks
+    half = size // 2
+    c = lax.axis_index("context"); m = lax.axis_size("context")
+    nxt, prv, cf = lax.rem(c + 1, m), lax.rem(c + m - 1, m), lax.rem(c + 2, m)
+    T = {"tensor": 1 - lax.axis_index("tensor")}
+    C = lambda i: {"context": i}
+    meet([T, C(nxt), C(prv)])
+    def copy(src, dst, k, to):
+        return pltpu.make_async_remote_copy(src, dst, send.at[k], recv.at[k], device_id=to, device_id_type=MESH)
+    def rows_of(owner, at, n):
+        return out_ref.at[pl.ds(pl.multiple_of(owner * rows + at, 16), n)]
+    started = []
+    for k in range(chunks):
+        at = pl.ds(k * size, size)
+        cp = copy(part_ref.at[at], other.at[at], k, T); cp.start(); started.append(cp)
+    locals_ = []
+    def forward(k):
+        a = rows_of(prv, k * size, size)
+        copy(a, a, chunks + k, C(prv)).wait_recv()
+        w = rows_of(prv, k * size, half)
+        cp = copy(w, w, 3 * chunks + k, C(nxt)); cp.start(); started.append(cp)
+        a = rows_of(nxt, k * size, size)
+        copy(a, a, 2 * chunks + k, C(nxt)).wait_recv()
+        w = rows_of(nxt, k * size + half, half)
+        cp = copy(w, w, 4 * chunks + k, C(prv)); cp.start(); started.append(cp)
+    for k in range(chunks):
+        at = pl.ds(k * size, size)
+        started[k].wait_recv()
+        mid = x_ref[at].astype(f32) + (part_ref[at].astype(f32) + other[at].astype(f32))
+        mid_ref[at] = mid
+        r = lax.rsqrt(jnp.mean(mid * mid, axis=-1, keepdims=True) + EPSILON)
+        normed[at] = (mid * r * gain_ref[...]).astype(bf16)
+        lc = pltpu.make_async_copy(normed.at[at], rows_of(c, k * size, size), local.at[k]); lc.start(); locals_.append(lc)
+        for d, to in ((0, nxt), (1, prv)):
+            cp = copy(normed.at[at], rows_of(c, k * size, size), (1 + d) * chunks + k, C(to)); cp.start(); started.append(cp)
+        if k:
+            forward(k - 1)
+    forward(chunks - 1)
+    for k in range(chunks):
+        w = rows_of(cf, k * size, half); copy(w, w, 3 * chunks + k, C(prv)).wait_recv()
+        w = rows_of(cf, k * size + half, half); copy(w, w, 4 * chunks + k, C(nxt)).wait_recv()
+    for cp in started: cp.wait_send()
+    for lc in locals_: lc.wait()
+
+def norm_gather(part, x, gain, cid=2):
+    rows, width = x.shape
+    return pl.pallas_call(norm_kernel,
+        out_shape=(jax.ShapeDtypeStruct((rows, width), f32), jax.ShapeDtypeStruct((4 * rows, width), bf16)),
+        in_specs=[VM] * 3, out_specs=(VM, ANY),
+        scratch_shapes=[pltpu.VMEM((rows, width), bf16), pltpu.VMEM((rows, width), bf16),
+                        pltpu.SemaphoreType.DMA((20,)), pltpu.SemaphoreType.DMA((20,)), pltpu.SemaphoreType.DMA((4,))],
+        compiler_params=pltpu.CompilerParams(collective_id=cid, has_side_effects=True), name="norm_gather")(part, x, gain[None])
+
+class Wire:
+    def __init__(self, send, recv):
+        self.send, self.recv, self.used, self.started = send, recv, 0, []
+
+    def push(self, src, dst, to):
+        k = self.used
+        self.used += 1
+        copy = pltpu.make_async_remote_copy(
+            src, dst, self.send.at[k], self.recv.at[k], device_id=to, device_id_type=MESH
+        )
+        copy.start()
+        self.started.append(copy)
+        return copy
+
+    def drain(self):
+        for copy in self.started:
+            copy.wait_send()
+
+
+def along_context():
+    c, m = lax.axis_index("context"), lax.axis_size("context")
+    return c, lax.rem(c + 1, m), lax.rem(c + m - 1, m), lax.rem(c + 2, m)
+
+
+def along_fsdp():
+    f, n = lax.axis_index("fsdp"), lax.axis_size("fsdp")
+    core = f + 1 - 2 * lax.rem(f, 2)
+    far = f + 2 - 4 * lax.rem(lax.div(f, 2), 2)
+    return f, core, far, lax.rem(f + 4, n), lax.rem(f + n - 4, n)
+
+
+class RowSum:
+    def __init__(self, wire, part, out, from_prv, from_nxt, mine, other, chunks):
+        self.wire, self.part, self.out, self.chunks = wire, part, out, chunks
+        self.from_prv, self.from_nxt, self.mine, self.other = from_prv, from_nxt, mine, other
+        self.rows, self.width = out.shape
+        self.half = self.rows // 2
+        self.c, self.nxt, self.prv, self.cf = along_context()
+        self.relay_p, self.relay_n, self.plain_p, self.plain_n = {}, {}, {}, {}
+        self.more_p, self.more_n, self.swap = {}, {}, {}
+
+    def cols(self, k):
+        size = self.width // self.chunks
+        return pl.ds(k * size, size)
+
+    def win(self, owner, second, k):
+        at = pl.multiple_of(owner * self.rows + second * self.half, 16)
+        return pl.ds(at, self.half), self.cols(k)
+
+    def start(self, k):
+        up, down = {"context": self.nxt}, {"context": self.prv}
+        part, cols = self.part, self.cols(k)
+        push = self.wire.push
+        self.relay_p[k] = push(part.at[self.win(self.cf, 0, k)], self.from_prv.at[0, :, cols], up)
+        self.relay_n[k] = push(part.at[self.win(self.cf, 1, k)], self.from_nxt.at[0, :, cols], down)
+        self.plain_p[k] = push(part.at[self.win(self.nxt, 1, k)], self.from_prv.at[1, :, cols], up)
+        self.plain_n[k] = push(part.at[self.win(self.prv, 0, k)], self.from_nxt.at[1, :, cols], down)
+
+    def relay(self, k):
+        cols, push = self.cols(k), self.wire.push
+        self.relay_p[k].wait_recv()
+        self.from_prv[0, :, cols] = (
+            self.from_prv[0, :, cols].astype(f32) + self.part[self.win(self.nxt, 0, k)].astype(f32)
+        ).astype(bf16)
+        self.more_p[k] = push(self.from_prv.at[0, :, cols], self.from_prv.at[2, :, cols], {"context": self.nxt})
+        self.relay_n[k].wait_recv()
+        self.from_nxt[0, :, cols] = (
+            self.from_nxt[0, :, cols].astype(f32) + self.part[self.win(self.prv, 1, k)].astype(f32)
+        ).astype(bf16)
+        self.more_n[k] = push(self.from_nxt.at[0, :, cols], self.from_nxt.at[2, :, cols], {"context": self.prv})
+
+    def exchange(self, k):
+        cols, half = self.cols(k), self.half
+        self.plain_n[k].wait_recv()
+        self.more_p[k].wait_recv()
+        first = (
+            self.part[self.win(self.c, 0, k)].astype(f32)
+            + self.from_nxt[1, :, cols].astype(f32)
+            + self.from_prv[2, :, cols].astype(f32)
+        )
+        self.mine[pl.ds(0, half), cols] = first.astype(bf16)
+        self.plain_p[k].wait_recv()
+        self.more_n[k].wait_recv()
+        second = (
+            self.part[self.win(self.c, 1, k)].astype(f32)
+            + self.from_prv[1, :, cols].astype(f32)
+            + self.from_nxt[2, :, cols].astype(f32)
+        )
+        self.mine[pl.ds(half, half), cols] = second.astype(bf16)
+        to = {"tensor": 1 - lax.axis_index("tensor")}
+        self.swap[k] = self.wire.push(self.mine.at[:, cols], self.other.at[:, cols], to)
+
+    def finish(self, k):
+        cols = self.cols(k)
+        self.swap[k].wait_recv()
+        total = self.mine[:, cols].astype(f32) + self.other[:, cols].astype(f32)
+        self.out[:, cols] = total.astype(self.out.dtype)
+
+
+class ShardSum:
+    def __init__(self, wire, got, from_down, from_up, pair, last, chunks):
+        self.wire, self.got, self.from_down, self.from_up = wire, got, from_down, from_up
+        self.pair, self.last, self.chunks = pair, last, chunks
+        self.shard, width = got.shape[1:]
+        self.half, self.size = self.shard // 2, width // chunks
+        self.f, self.core, self.far, self.up, self.down = along_fsdp()
+        self.side = lax.rem(lax.div(self.f, 2), 2)
+        self.mine = lax.rem(self.f, 2)
+        self.cores, self.plain, self.relay, self.more, self.cross = {}, {}, {}, {}, {}
+
+    def cols(self, k):
+        return pl.ds(k * self.size, self.size)
+
+    def send_core(self, k, rel, src):
+        self.cores[k, rel] = self.wire.push(
+            src, self.got.at[pl.ds(2 * rel, 2), :, self.cols(k)], {"fsdp": self.core}
+        )
+
+    def add_core(self, k, rel, own):
+        self.cores[k, rel].wait_recv()
+        at = pl.ds(2 * rel, 2), slice(None), self.cols(k)
+        self.got[at] = (self.got[at].astype(f32) + own.astype(f32)).astype(bf16)
+
+    def block(self, rel, second, k):
+        return pl.ds(2 * rel, 2), pl.ds(second * self.half, self.half), self.cols(k)
+
+    def start(self, k):
+        got, cols, push = self.got, self.cols(k), self.wire.push
+        up, down = {"fsdp": self.up}, {"fsdp": self.down}
+        self.relay[k] = (
+            push(got.at[self.block(2, 0, k)], self.from_down.at[0, :, :, cols], up),
+            push(got.at[self.block(2, 1, k)], self.from_up.at[0, :, :, cols], down),
+        )
+        self.plain[k] = (
+            push(got.at[self.block(1, 1, k)], self.from_down.at[1, :, :, cols], up),
+            push(got.at[self.block(3, 0, k)], self.from_up.at[1, :, :, cols], down),
+        )
+
+    def relays(self, k):
+        cols, push = self.cols(k), self.wire.push
+        self.relay[k][0].wait_recv()
+        at = (0, slice(None), slice(None), cols)
+        self.from_down[at] = (
+            self.from_down[at].astype(f32) + self.got[self.block(1, 0, k)].astype(f32)
+        ).astype(bf16)
+        one = push(self.from_down.at[at], self.from_down.at[2, :, :, cols], {"fsdp": self.up})
+        self.relay[k][1].wait_recv()
+        self.from_up[at] = (
+            self.from_up[at].astype(f32) + self.got[self.block(3, 1, k)].astype(f32)
+        ).astype(bf16)
+        two = push(self.from_up.at[at], self.from_up.at[2, :, :, cols], {"fsdp": self.down})
+        self.more[k] = (one, two)
+
+    def across(self, k):
+        cols, half = self.cols(k), self.half
+        self.more[k][0].wait_recv()
+        self.plain[k][1].wait_recv()
+        self.pair[:, pl.ds(0, half), cols] = (
+            self.got[self.block(0, 0, k)].astype(f32)
+            + self.from_down[2, :, :, cols].astype(f32)
+            + self.from_up[1, :, :, cols].astype(f32)
+        ).astype(bf16)
+        self.more[k][1].wait_recv()
+        self.plain[k][0].wait_recv()
+        self.pair[:, pl.ds(half, half), cols] = (
+            self.got[self.block(0, 1, k)].astype(f32)
+            + self.from_down[1, :, :, cols].astype(f32)
+            + self.from_up[2, :, :, cols].astype(f32)
+        ).astype(bf16)
+        self.cross[k] = self.wire.push(
+            self.pair.at[1 - self.side, :, cols], self.last.at[:, cols], {"fsdp": self.far}
+        )
+
+    def total(self, k):
+        cols = self.cols(k)
+        self.cross[k].wait_recv()
+        return self.pair[self.side, :, cols].astype(f32) + self.last[:, cols].astype(f32)
+
+
+def shard_scratch(shard, width, blocks=8):
+    return [
+        pltpu.VMEM((blocks, shard, width), bf16),
+        pltpu.VMEM((3, 2, shard // 2, width), bf16),
+        pltpu.VMEM((3, 2, shard // 2, width), bf16),
+        pltpu.VMEM((2, shard, width), bf16),
+        pltpu.VMEM((shard, width), bf16),
+    ]
+
+
+def row_scratch(rows, width):
+    return [pltpu.VMEM((3, rows // 2, width), bf16)] * 2 + [pltpu.VMEM((rows, width), bf16)] * 2
+
+
+def everyone_near():
+    _, core, far, up, down = along_fsdp()
+    _, nxt, prv, _ = along_context()
+    return [{"fsdp": i} for i in (core, far, up, down)] + [
+        {"context": nxt}, {"context": prv}, {"tensor": 1 - lax.axis_index("tensor")}
+    ]
+
+
+ORDER = (2, 1, 3, 0)
+
+
+def mlp_back_kernel(
+    normed_ref, dy_ref, gate_ref, lift_ref, hidden_ref, first_ref, second_ref,
+    first_out, second_out, shard_out,
+    grads, got, from_down, from_up, pair, last,
+    prv1, nxt1, mine1, other1, prv2, nxt2, mine2, other2, send, recv,
+):
+    wire = Wire(send, recv)
+    meet(everyone_near())
+    chunks = 3
+    sums = ShardSum(wire, got, from_down, from_up, pair, last, chunks)
+    rows1 = RowSum(wire, first_ref, first_out, prv1, nxt1, mine1, other1, chunks)
+    rows2 = RowSum(wire, second_ref, second_out, prv2, nxt2, mine2, other2, chunks)
+    shard, span = sums.shard, sums.size
+    z = lax.div(sums.f, 4)
+    for k in range(chunks):
+        rows1.start(k)
+    pairs = ((normed_ref, gate_ref), (normed_ref, lift_ref), (dy_ref, hidden_ref))
+    for k, (left, right) in enumerate(pairs):
+        for rel in ORDER:
+            at = pl.multiple_of(lax.rem(z + rel, 4) * (4 * shard), 4 * shard)
+            tile = jnp.dot(left[pl.ds(at, 4 * shard), :], right[...], preferred_element_type=f32).astype(bf16)
+            for side in range(2):
+                for core in range(2):
+                    lo = (2 * side + core) * shard
+                    grads[core, 2 * rel + side, :, sums.cols(k)] = tile[lo : lo + shard]
+            sums.send_core(k, rel, grads.at[1 - sums.mine, pl.ds(2 * rel, 2), :, sums.cols(k)])
+        if k == 1:
+            for j in range(chunks):
+                rows1.relay(j)
+            for j in range(chunks):
+                rows2.start(j)
+        if k >= 1:
+            for rel in ORDER:
+                sums.add_core(k - 1, rel, grads[sums.mine, pl.ds(2 * rel, 2), :, sums.cols(k - 1)])
+            sums.start(k - 1)
+    for rel in ORDER:
+        sums.add_core(2, rel, grads[sums.mine, pl.ds(2 * rel, 2), :, sums.cols(2)])
+    sums.start(2)
+    for k in range(chunks):
+        rows1.exchange(k)
+        sums.relays(k)
+    for k in range(chunks):
+        rows2.relay(k)
+    for k in range(chunks):
+        rows1.finish(k)
+        sums.across(k)
+    for k in range(chunks):
+        rows2.exchange(k)
+    for k in range(chunks):
+        shard_out[:, sums.cols(k)] = sums.total(k).astype(bf16)
+        rows2.finish(k)
+    wire.drain()
+
+
+def mlp_back(normed_turned, dy_turned, d_gate, d_lift, hidden, first, second, cid=3):
+    width = normed_turned.shape[0]
+    rows, span = first.shape[0] // 4, d_gate.shape[1]
+    shard = width // 16
+    sems = 3 * (4 + 4 + 2 + 1) + 2 * 3 * 7
+    return pl.pallas_call(
+        mlp_back_kernel,
+        out_shape=(
+            jax.ShapeDtypeStruct((rows, width), f32),
+            jax.ShapeDtypeStruct((rows, width), bf16),
+            jax.ShapeDtypeStruct((shard, 3 * span), bf16),
+        ),
+        in_specs=[VM] * 7,
+        out_specs=(VM,) * 3,
+        scratch_shapes=[pltpu.VMEM((2, 8, shard, 3 * span), bf16)]
+        + shard_scratch(shard, 3 * span)
+        + row_scratch(rows, width) * 2
+        + [pltpu.SemaphoreType.DMA((sems,)), pltpu.SemaphoreType.DMA((sems,))],
+        compiler_params=pltpu.CompilerParams(
+            collective_id=cid, has_side_effects=True, vmem_limit_bytes=62 << 20
+        ),
+        name="mlp_back",
+    )(normed_turned, dy_turned, d_gate, d_lift, hidden, first, second)
 
 
 def rms_norm(values, gain_vec):
@@ -58,6 +499,26 @@
     low = x.astype(jnp.bfloat16)
     other = lax.ppermute(low, axis, [(0, 1), (1, 0)])
     return low.astype(jnp.float32) + other.astype(jnp.float32)
+
+
+def around(x):
+    size, rank = lax.axis_size("context"), lax.axis_index("context")
+    parts = [x] + [
+        lax.ppermute(x, "context", [(i, (i - k) % size) for i in range(size)]) for k in range(1, size)
+    ]
+    twice = jnp.concatenate(parts + parts, axis=0)
+    rows = x.shape[0]
+    return lax.dynamic_slice_in_dim(twice, (size - rank) % size * rows, size * rows)
+
+
+def back_around(x):
+    size, rank = lax.axis_size("context"), lax.axis_index("context")
+    rows = x.shape[0] // size
+    total = lax.dynamic_slice_in_dim(x, rank * rows, rows)
+    for k in range(1, size):
+        block = lax.dynamic_slice_in_dim(x, (rank + k) % size * rows, rows)
+        total = total + lax.ppermute(block, "context", [(i, (i + k) % size) for i in range(size)])
+    return total
 
 
 def hidden_range(width, parts, rank):
@@ -84,7 +545,6 @@
     w_up,
     w_down,
 ):
-    bf16, f32 = jnp.bfloat16, jnp.float32
     row_count, width = tokens.shape
     context_size = lax.axis_size("context")
     context_rank = lax.axis_index("context")
@@ -113,7 +573,8 @@
     mlp_pack = jnp.concatenate(
         [lax.dynamic_slice_in_dim(w, start, span, axis=1) for w in (w_gate, w_up, w_down.T)], axis=1
     )
-    attn_full = lax.all_gather(attn_pack, "fsdp", axis=0, tiled=True)
+    attn_full, dy_group = gather(attn_pack, cotangent)
+    mlp_pack, attn_full = lax.optimization_barrier((mlp_pack, attn_full))
     mlp_full = lax.all_gather(mlp_pack, "fsdp", axis=0, tiled=True)
     lin_cols = query_cols + 2 * kv_cols
     lin_full = attn_full[:, :lin_cols]
@@ -124,7 +585,6 @@
     keep = (
         jnp.arange(span) >= jnp.where(context_rank == context_size - 1, overlap, 0)
     )[None, :]
-    dy_group = lax.all_gather(cotangent, "context", axis=0, tiled=True)
 
     inputs = tokens.astype(f32)
     normed_one = rms_norm(inputs, gain_one).astype(bf16)
@@ -137,9 +597,7 @@
     query_heads = query_heads.reshape(row_count, heads_kv, per_group, HD)
     key_heads = rotate(key_lin.reshape(row_count, heads_kv, HD), cosine, sine_table).astype(bf16)
     value_heads = value_lin.astype(bf16).reshape(row_count, heads_kv, HD)
-    kv_group = lax.all_gather(
-        jnp.concatenate([key_heads, value_heads], axis=1), "context", axis=0, tiled=True
-    )
+    kv_group = around(jnp.concatenate([key_heads, value_heads], axis=1))
     key_group, value_group = kv_group[:, :heads_kv], kv_group[:, heads_kv:]
     scores = (
         jnp.einsum("qgjd,kgd->gjqk", query_heads, key_group, preferred_element_type=f32)
@@ -152,10 +610,8 @@
     probs_low = probs.astype(bf16)
     mixed = jnp.einsum("gjqk,kgd->qgjd", probs_low, value_group, preferred_element_type=f32)
     mixed = mixed.reshape(row_count, heads_query * HD).astype(bf16)
-    middle = inputs + swap_sum(tail_dot(mixed, out_turned), "tensor")
-    normed_two = rms_norm(middle, gain_two).astype(bf16)
-
-    normed_group = lax.all_gather(normed_two, "context", axis=0, tiled=True)
+
+    middle, normed_group = norm_gather(tail_dot(mixed, out_turned).astype(bf16), tokens, gain_two)
     d_hidden = jnp.dot(dy_group, down_turned, preferred_element_type=f32)
     gate_lin = jnp.dot(normed_group, gate_full, preferred_element_type=f32)
     lift_lin = jnp.dot(normed_group, lift_full, preferred_element_type=f32)
@@ -167,25 +623,11 @@
     ).astype(bf16)
     d_lift = jnp.where(keep, d_hidden * swish, 0.0).astype(bf16)
     d_normed_part = tail_dot(d_gate, gate_full) + tail_dot(d_lift, lift_full)
-    d_normed_two = swap_sum(
-        lax.psum_scatter(d_normed_part.astype(bf16), "context", scatter_dimension=0, tiled=True),
-        "tensor",
-    )
-    mlp_part = tail_dot(hidden, down_turned)
-    mlp_branch = swap_sum(
-        lax.psum_scatter(mlp_part.astype(bf16), "context", scatter_dimension=0, tiled=True),
-        "tensor",
-    )
-    result = (middle + mlp_branch).astype(bf16)
-    mlp_grads = jnp.concatenate(
-        [
-            lead_dot(normed_group, d_gate).astype(bf16),
-            lead_dot(normed_group, d_lift).astype(bf16),
-            lead_dot(dy_group, hidden).astype(bf16),
-        ],
-        axis=1,
-    )
-    mlp_shard = lax.psum_scatter(mlp_grads, "fsdp", scatter_dimension=0, tiled=True)
+    mlp_part = tail_dot(hidden, down_turned).astype(bf16)
+    d_normed_two, mlp_branch, mlp_shard = mlp_back(
+        normed_group.T, dy_group.T, d_gate, d_lift, hidden, d_normed_part.astype(bf16), mlp_part
+    )
+    result = (middle + mlp_branch.astype(f32)).astype(bf16)
     mlp_all = lax.all_gather(mlp_shard, "context", axis=0)
 
     def whole(k):
@@ -214,9 +656,7 @@
         * score_scale
     )
     d_value_part = jnp.einsum("gjqk,qgjd->kgd", probs_low, d_mixed, preferred_element_type=f32)
-    d_kv = lax.psum_scatter(
-        jnp.concatenate([d_key_part, d_value_part], axis=1), "context", scatter_dimension=0, tiled=True
-    )
+    d_kv = back_around(jnp.concatenate([d_key_part, d_value_part], axis=1))
     d_key, d_value = d_kv[:, :heads_kv], d_kv[:, heads_kv:]
 
     def turn_query(values):
@@ -245,8 +685,11 @@
     _, pull_one = jax.vjp(rms_norm, inputs, gain_one)
     d_input_norm, grad_gain_attn = pull_one(d_normed_one)
     grad_tokens = d_middle + d_input_norm
-    small = lax.psum(
-        jnp.concatenate([grad_gain_attn, grad_gain_mlp, bias_part]), ("fsdp", "context")
+    small = jnp.sum(
+        lax.all_gather(
+            jnp.concatenate([grad_gain_attn, grad_gain_mlp, bias_part])[None], ("fsdp", "context"), axis=0, tiled=True
+        ),
+        axis=0,
     )
     own = lambda at: lax.dynamic_slice_in_dim(small, at + fsdp_rank * shard, shard)
     bias_total = small[2 * width :]

time: 1020 us -> 604 us (0.59)
  blocking collectives: 341 us -> 0 us
  waiting for transfers between devices: 440 us -> 225 us
  Pallas kernels: 0 us -> 188 us
  matrix products: 93.3 us -> 71.5 us
  other arithmetic: 52.8 us -> 32.1 us
    psum x1 -> x0, blocking collectives: 325 us -> none  [on_device(): lax.psum(jnp.concatenate([grad_gain_attn, grad_gain_mlp, bias_part]), ('f...]
    reduce_scatter x4 -> x0, waiting for transfers between devices: 190 us -> none  [the longest x1 114 us: on_device(): lax.psum_scatter(mlp_grads, 'fsdp', scatter_dimension=0, tiled=True)]
    pallas_call x0 -> x3, Pallas kernels: none -> 188 us  [the longest x1 94.7 us: mlp_back(): pl.pallas_call(mlp_back_kernel, out_shape=(jax.ShapeDtypeStruct((rows, wi...]
    all_gather x1, waiting for transfers between devices: 69.2 us -> 0.02 us  [on_device(): mlp_full = lax.all_gather(mlp_pack, 'fsdp', axis=0, tiled=True)]
    unnamed x12 -> x6, waiting for transfers between devices: 39 us -> 86.2 us
    all_gather x3 -> x1, waiting for transfers between devices: 90.6 us -> 46.6 us  [on_device(): lax.all_gather(jnp.concatenate([grad_gain_attn, grad_gain_mlp, bias_part]...]
    psum x1, waiting for transfers between devices: 0.01 us -> 40.3 us  [on_device(): lax.psum(lax.psum_scatter(attn_grads, 'fsdp', scatter_dimension=0, tiled=...]
    ppermute x4 -> x1, waiting for transfers between devices: 51 us -> 13.7 us  [swap_sum(): other = lax.ppermute(low, axis, [(0, 1), (1, 0)])]
  transfers between devices with their start and end apart: 15 -> 12, of which waited for: 11 -> 7; matrix products, arithmetic and copies ran while one was open for 12% -> 12% of each run, Pallas kernels for 0% -> 9%
where the time goes in v2:
time: 604 us; the launch traced here: 598 us
  waiting for transfers between devices  225 us (37%)
  Pallas kernels  188 us (31%)
  matrix products  71.5 us (12%)
  local copies, waits for them, and re-layouts  55.3 us (9%)
  other arithmetic  32.1 us (5%)
  between operations  15 us (2%)
  starting transfers between devices  11 us (2%)
    pallas_call x1, Pallas kernels, mlp_back(): pl.pallas_call(mlp_back_kernel, out_shape=(jax.ShapeDtypeStruct((rows, wi...  94.7 us
    unnamed x6, waiting for transfers between devices  86.2 us
    pallas_call x1, Pallas kernels, norm_gather(): pl.pallas_call(norm_kernel, out_shape=(jax.ShapeDtypeStruct((rows, width)...  52.5 us
    all_gather x1, waiting for transfers between devices, on_device(): lax.all_gather(jnp.concatenate([grad_gain_attn, grad_gain_mlp, bias_part]...  46.6 us
    pallas_call x1, Pallas kernels, gather(): pl.pallas_call(gather_kernel, out_shape=(jax.ShapeDtypeStruct((16 * shard...  40.7 us
    psum x1, waiting for transfers between devices, on_device(): lax.psum(lax.psum_scatter(attn_grads, 'fsdp', scatter_dimension=0, tiled=...  40.3 us
    all_gather x1, waiting for transfers between devices, on_device(): mlp_all = lax.all_gather(mlp_shard, 'context', axis=0)  30.8 us
    unnamed x99, local copies, waits for them, and re-layouts  26.8 us
  transfers between devices with their start and end apart: 12, of which 7 were waited for; matrix products, arithmetic and copies ran while one was open for 12% of the time, Pallas kernels for 9%

profile of v2, /device:TPU:0, one launch (start us, length us, event | category | flops | bytes accessed | tf_op | source)
XLA Modules:
  0.0 597.6 jit_solution(10719757865875253930)
XLA Ops:
  7.3 1.0 constant_dynamic-update-slice_fusion.3
  9.3 1.3 constant_dynamic-slice_fusion
  13.7 40.7 %gather_rows.1 = (bf16[1536,1920]{1,0:T(8,128)(2,1)}, bf16[1024,1536]{1,0:T(8,128)(2,1)}) custom-call(bf16[96,1920]{1,0:T(8,128)(2,1)} %copy-done.26, bf16[256,1536]{1,0:T(8,128)(2,1)} %y_ref.1), custom_call_target="tpu_custom_call" | custom-call | tf_op jit(solution)/shard_map/gather_rows/pallas_call | solution.py:110
  56.3 1.8 convert_reduce_fusion.1
  58.4 2.9 fusion.42
  63.0 3.0 collective-permute-start
  66.6 1.0 collective-permute-start.2
  68.2 1.2 copy.115
  70.2 1.0 mul.277
  71.1 1.1 copy.112
  73.1 2.3 add_convert_fusion.4
  75.3 0.9 fusion.57
  76.4 1.2 copy.116
  78.1 4.9 copy.121
  83.1 0.9 constant_dynamic-update-slice_fusion.10
  88.7 1.1 fusion.5
  89.8 1.3 fusion.4
  91.1 1.3 copy-done.2
  92.5 1.9 fusion.49
  94.4 3.5 convolution_convert_fusion.3.part_ref
  97.9 52.5 %norm_gather.1 = (f32[256,1536]{1,0:T(8,128)}, bf16[1024,1536]{1,0:T(8,128)(2,1)}) custom-call(bf16[256,1536]{1,0:T(8,128)(2,1)} %convolution_convert_fusion.3.part_ref, bf16[256,1536]{1,0:T(8,128)(2,1)} %x_ref.1, f32[1,1536]{1,0:T(1,128)} %reshape.273.gain_ref), custom_call_target="tpu_custom_call" | custom-call | tf_op jit(solution)/shard_map/norm_gather/pallas_call | solution.py:165
  150.5 5.0 copy.120
  155.7 7.3 %fusion.14 = f32[1024,1152]{1,0:T(8,128)S(1)} fusion(bf16[1024,1536]{1,0:T(8,128)(2,1)} %get-tuple-element.26, bf16[1536,3456]{1,0:T(8,128)(2,1)} %all-gather.6.cloned.1.call-done), kind=kOutput, calls=%fused_computation.27 | convolution fusion | flops 3623878656 | bytes 11403264 | tf_op jit(solution)/shard_map/dot_general | solution.py:616
  163.0 5.9 fusion.20
  169.0 9.2 %select_convert_fusion = (bf16[1024,1152]{1,0:T(8,128)(2,1)S(1)}, bf16[1024,1152]{1,0:T(8,128)(2,1)S(1)}, bf16[1024,1152]{1,0:T(8,128)(2,1)S(1)}) fusion(pred[1152]{0:T(1024)(128)(4,1)S(1)} %iota_compare_fusion.2, f32[1024,1152]{1,0:T(8,128)S(1)} %fusion.14, f32[1024,1152]{1,0:T(8,128)} %fusion.20, bf16[1024,1536]{1,0:T(8,128)(2,1)S(1)} %copy-done.13, ...), kind=kOutput, calls=%fused_computation.12 | convolution fusion | flops 3645112320 | bytes 23201792 | tf_op jit(solution)/shard_map/dot_general | solution.py:617
  178.2 5.8 convolution_convert_fusion.1.second_ref
  184.0 6.2 %fusion.12 = f32[1024,1536]{1,0:T(8,128)} fusion(bf16[1024,1152]{1,0:T(8,128)(2,1)S(1)} %get-tuple-element.97.gate_ref, bf16[1536,3456]{1,0:T(8,128)(2,1)S(1)} %copy-done.39), kind=kOutput, calls=%fused_computation.25 | convolution fusion | flops 3623878656 | bytes 12189696 | tf_op jit(solution)/shard_map/dot_general | solution.py:493
  190.2 7.7 %add_convert_fusion.first_ref = bf16[1024,1536]{1,0:T(8,128)(2,1)} fusion(f32[1024,1536]{1,0:T(8,128)} %fusion.12, bf16[1024,1152]{1,0:T(8,128)(2,1)S(1)} %get-tuple-element.98.lift_ref, bf16[1536,3456]{1,0:T(8,128)(2,1)S(1)} %copy-done.39), kind=kOutput, calls=%fused_computation.6 | convolution fusion | flops 3627024384 | bytes 15335424 | tf_op jit(solution)/shard_map/dot_general | solution.py:493
  197.9 94.7 %mlp_back.1 = (f32[256,1536]{1,0:T(8,128)}, bf16[256,1536]{1,0:T(8,128)(2,1)}, bf16[96,3456]{1,0:T(8,128)(2,1)}) custom-call(bf16[1536,1024]{1,0:T(8,128)(2,1)} %bitcast.181, bf16[1536,1024]{1,0:T(8,128)(2,1)} %bitcast.180, bf16[1024,1152]{1,0:T(8,128)(2,1)} %copy-done.16, bf16[1024,1152]{1,0:T(8,128)(2,1)} %copy-done.17, bf16[1024,1152]{1,0:T(8,128)(2,1)} %copy-done.15, ...), custom_call_target="tpu_custom_call" | custom-call | tf_op jit(solution)/shard_map/mlp_back/pallas_call | solution.py:435
  292.7 2.4 multiply_reduce_fusion
  295.5 2.8 fusion.37
  298.3 1.1 copy-done.3
  299.4 3.4 fusion.46
  302.8 1.9 copy.122
  304.7 5.2 fusion
  310.0 1.7 fusion.52
  311.7 2.0 fusion.7
  313.7 1.6 broadcast_multiply_fusion
  315.4 1.0 fusion.56
  316.5 3.4 collective-permute-start.3
  319.9 1.6 collective-permute-start.4
  321.4 1.2 collective-permute-start.5
  322.8 4.3 collective-permute-done.3
  327.2 2.9 collective-permute-done.4
  330.8 3.0 fusion.26
  333.9 1.3 convert_reduce_fusion
  335.2 13.7 %collective-permute-done.6 = bf16[256,1536]{1,0:T(8,128)(2,1)S(1)} collective-permute-done((bf16[256,1536]{1,0:T(8,128)(2,1)S(1)}, bf16[256,1536]{1,0:T(8,128)(2,1)S(1)}, u32[]{:S(2)}, u32[]{:S(2)}) %collective-permute-start.6) | collective-permute-done | bytes 786464 | tf_op jit(solution)/shard_map/ppermute | solution.py:500
  352.1 1.8 convolution_convert_fusion.2
  353.9 2.1 convolution_convert_fusion
  356.0 2.7 pad_maximum_fusion
  358.7 8.3 %copy.150 = bf16[1536,1792]{1,0:T(8,128)(2,1)} copy(bf16[1536,1792]{0,1:T(8,128)(2,1)} %pad_maximum_fusion) | data formatting | bytes 11010048
  367.7 2.9 fusion.38
  370.6 46.6 %all-gather.8.cloned.1.call-done = f32[262144]{0:T(1024)} async-done(((f32[4096]{0:T(1024)}), f32[262144]{0:T(1024)}) %all-gather.8.cloned.1.call-update) | async-done | bytes 1048592 | tf_op jit(solution)/shard_map/all_gather | solution.py:689
  417.1 1.4 reshape.275
  420.3 30.8 %all-gather.10.cloned.1.call-done = bf16[384,3456]{1,0:T(8,128)(2,1)} async-done(((bf16[96,3456]{1,0:T(8,128)(2,1)}), bf16[384,3456]{1,0:T(8,128)(2,1)}) %all-gather.10.cloned.1.call-update) | async-done | bytes 2654224 | tf_op jit(solution)/shard_map/all_gather | solution.py:631
  451.1 2.1 slice_bitcast_fusion.4
  453.2 1.3 convert_bitcast_fusion
  454.5 1.3 maximum_convert_fusion.1
  455.8 85.4 %reduce-scatter.4.cloned.1.call-done = bf16[96,1792]{1,0:T(8,128)(2,1)} async-done(((bf16[1536,1792]{1,0:T(8,128)(2,1)}), bf16[96,1792]{1,0:T(8,128)(2,1)}) %reduce-scatter.4.cloned.1.call-update) | async-done | bytes 344080
  541.2 2.0 copy.151
  543.2 1.3 maximum_convert_fusion
  544.5 40.3 %all-reduce.7.cloned.1.call-done = bf16[96,1792]{0,1:T(8,128)(2,1)} async-done(((bf16[96,1792]{0,1:T(8,128)(2,1)}), bf16[96,1792]{0,1:T(8,128)(2,1)}) %all-reduce.7.cloned.1.call-update) | async-done | bytes 344080 | tf_op jit(solution)/shard_map/psum | solution.py:681
  584.8 1.1 convert_element_type.195
  586.8 1.0 slice.178
  (167 shorter events, 27.1 us)
Async XLA Ops:
  7.2 2.0 copy-start
  7.2 48.2 %copy-start.38 = (s32[1,3]{1,0:T(1,128)S(1)}, s32[1,3]{1,0:T(1,128)}, u32[]{:S(2)}) copy-start(s32[1,3]{1,0:T(1,128)} %param.17) | copy-start | bytes 40
  7.2 49.1 %copy-start.35 = (bf16[768]{0:T(1024)(128)(2,1)S(1)}, bf16[768]{0:T(1024)(128)(2,1)}, u32[]{:S(2)}) copy-start(bf16[768]{0:T(1024)(128)(2,1)} %param.20) | copy-start | bytes 4612
  7.2 49.1 %copy-start.37 = (bf16[128]{0:T(256)(128)(2,1)S(1)}, bf16[128]{0:T(256)(128)(2,1)}, u32[]{:S(2)}) copy-start(bf16[128]{0:T(256)(128)(2,1)} %param.22) | copy-start | bytes 772
  7.2 49.1 %copy-start.36 = (bf16[128]{0:T(256)(128)(2,1)S(1)}, bf16[128]{0:T(256)(128)(2,1)}, u32[]{:S(2)}) copy-start(bf16[128]{0:T(256)(128)(2,1)} %param.24) | copy-start | bytes 772
  7.2 50.9 %copy-start.7 = (bf16[256,1536]{1,0:T(8,128)(2,1)S(1)}, bf16[256,1536]{1,0:T(8,128)(2,1)}, u32[]{:S(2)}) copy-start(bf16[256,1536]{1,0:T(8,128)(2,1)} %x_ref.1) | copy-start | bytes 2359300
  7.2 148.4 %all-gather.6.cloned.1.call-start = ((), (), s32[]{:S(2)}) async-start(), calls=%async_computation.1 | async-start | bytes 11280384 | tf_op jit(solution)/shard_map/all_gather | solution.py:578
  13.0 0.7 copy-start.26
  55.3 361.8 %all-gather.8.cloned.1.call-start = ((), (), s32[]{:S(2)}) async-start(), calls=%async_computation.3 | async-start | bytes 1064960 | tf_op jit(solution)/shard_map/all_gather | solution.py:689
  58.4 3.0 copy-start.33
  58.4 3.0 copy-start.31
  61.9 5.7 copy-start.20
  61.9 5.7 copy-start.22
  63.0 20.1 %collective-permute-start = (bf16[256,2,128]{2,0,1:T(8,128)(2,1)}, bf16[256,2,128]{2,0,1:T(8,128)(2,1)}, u32[]{:S(2)}, u32[]{:S(2)}) collective-permute-start(bf16[256,2,128]{2,0,1:T(8,128)(2,1)} %get-tuple-element.127), channel_id=1, source_target_pairs={{0,6},{2,0},{4,2},{6,4},{1,7},{3,1},{5,3},{7,5},{8,14},{10,8},{12,... | collective-permute-start | bytes 393224 | tf_op jit(solution)/shard_map/ppermute | solution.py:507
  66.0 18.0 %collective-permute-start.1 = (bf16[256,2,128]{2,0,1:T(8,128)(2,1)}, bf16[256,2,128]{2,0,1:T(8,128)(2,1)}, u32[]{:S(2)}, u32[]{:S(2)}) collective-permute-start(bf16[256,2,128]{2,0,1:T(8,128)(2,1)} %get-tuple-element.127), channel_id=1, source_target_pairs={{0,4},{2,6},{4,0},{6,2},{1,5},{3,7},{5,1},{7,3},{8,12},{10,14},{12... | collective-permute-start | bytes 393224 | tf_op jit(solution)/shard_map/ppermute | solution.py:507
  66.6 18.3 %collective-permute-start.2 = (bf16[256,2,128]{2,0,1:T(8,128)(2,1)}, bf16[256,2,128]{2,0,1:T(8,128)(2,1)}, u32[]{:S(2)}, u32[]{:S(2)}) collective-permute-start(bf16[256,2,128]{2,0,1:T(8,128)(2,1)} %get-tuple-element.127), channel_id=1, source_target_pairs={{0,2},{2,4},{4,6},{6,0},{1,3},{3,5},{5,7},{7,1},{8,10},{10,12},{12... | collective-permute-start | bytes 393224 | tf_op jit(solution)/shard_map/ppermute | solution.py:507
  67.8 1.6 copy-start.24
  68.2 7.1 %copy-start.9 = (f32[256,6,128]{0,2,1:T(8,128)}, f32[256,6,128]{0,2,1:T(8,128)S(1)}, u32[]{:S(2)}) copy-start(f32[256,6,128]{0,2,1:T(8,128)S(1)} %maximum_multiply_fusion) | copy-start | bytes 2359300
  78.1 4.9 copy-start.27
  88.7 2.4 copy-start.28
  89.8 2.7 copy-start.2
  94.4 56.0 %copy-start.29 = (bf16[128,6,256]{2,0,1:T(8,128)(2,1)}, bf16[128,6,256]{2,0,1:T(8,128)(2,1)S(1)}, u32[]{:S(2)}) copy-start(bf16[128,6,256]{2,0,1:T(8,128)(2,1)S(1)} %fusion.49) | copy-start | bytes 1179652
  150.5 5.0 copy-start.5
  155.6 7.3 %copy-start.12 = (bf16[1024,1536]{1,0:T(8,128)(2,1)S(1)}, bf16[1024,1536]{1,0:T(8,128)(2,1)}, u32[]{:S(2)}) copy-start(bf16[1024,1536]{1,0:T(8,128)(2,1)} %get-tuple-element.27) | copy-start | bytes 9437188
  155.7 7.3 %copy-start.39 = (bf16[1536,3456]{1,0:T(8,128)(2,1)S(1)}, bf16[1536,3456]{1,0:T(8,128)(2,1)}, u32[]{:S(2)}) copy-start(bf16[1536,3456]{1,0:T(8,128)(2,1)} %all-gather.6.cloned.1.call-done) | copy-start | bytes 31850500
  163.0 5.9 copy-start.13
  178.2 5.8 copy-start.15
  178.2 5.8 copy-start.16
  178.2 12.0 %copy-start.17 = (bf16[1024,1152]{1,0:T(8,128)(2,1)}, bf16[1024,1152]{1,0:T(8,128)(2,1)S(1)}, u32[]{:S(2)}) copy-start(bf16[1024,1152]{1,0:T(8,128)(2,1)S(1)} %get-tuple-element.98.lift_ref) | copy-start | bytes 7077892
  292.7 2.4 copy-start.6
  292.7 2.8 copy-start.11
  298.3 1.1 copy-start.3
  299.4 10.5 %slice-start = ((s8[6291456]{0:T(1024)(128)(4,1)}), s8[2097152]{0:T(1024)(128)(4,1)S(1)}, s32[]{:S(2)}) async-start(s8[6291456]{0:T(1024)(128)(4,1)} %bitcast.178), calls=%async_computation.6 | async-start | bytes 4194304
  304.7 5.2 slice-start.1
  304.7 5.3 copy-start.30
  311.7 2.0 copy-start.25
  313.7 1.7 copy-start.10
  313.7 1.7 copy-start.18
  316.5 13.7 %copy-start.21 = (f32[256,64]{1,0:T(8,128)S(1)}, f32[256,64]{1,0:T(8,128)}, u32[]{:S(2)}) copy-start(f32[256,64]{1,0:T(8,128)} %copy-done.20) | copy-start | bytes 196612
  316.5 10.7 %collective-permute-start.3 = (f32[256,2,128]{2,0,1:T(8,128)S(1)}, f32[256,2,128]{2,0,1:T(8,128)S(1)}, u32[]{:S(2)}, u32[]{:S(2)}) collective-permute-start(f32[256,2,128]{2,0,1:T(8,128)S(1)} %get-tuple-element.113), channel_id=1, source_target_pairs={{0,2},{2,4},{4,6},{6,0},{1,3},{3,5},{5,7},{7,1},{8,10},{10,12},{12... | collective-permute-start | bytes 786440 | tf_op jit(solution)/shard_map/ppermute | solution.py:520
  319.9 10.2 %collective-permute-start.4 = (f32[256,2,128]{2,0,1:T(8,128)S(1)}, f32[256,2,128]{2,0,1:T(8,128)S(1)}, u32[]{:S(2)}, u32[]{:S(2)}) collective-permute-start(f32[256,2,128]{2,0,1:T(8,128)S(1)} %get-tuple-element.114), channel_id=1, source_target_pairs={{0,4},{2,6},{4,0},{6,2},{1,5},{3,7},{5,1},{7,3},{8,12},{10,14},{12... | collective-permute-start | bytes 786440 | tf_op jit(solution)/shard_map/ppermute | solution.py:520
  321.4 8.7 %collective-permute-start.5 = (f32[256,2,128]{2,0,1:T(8,128)S(1)}, f32[256,2,128]{2,0,1:T(8,128)S(1)}, u32[]{:S(2)}, u32[]{:S(2)}) collective-permute-start(f32[256,2,128]{2,0,1:T(8,128)S(1)} %get-tuple-element.115), channel_id=1, source_target_pairs={{0,6},{2,0},{4,2},{6,4},{1,7},{3,1},{5,3},{7,5},{8,14},{10,8},{12,... | collective-permute-start | bytes 786440 | tf_op jit(solution)/shard_map/ppermute | solution.py:520
  322.6 7.7 %copy-start.23 = (f32[256,64]{1,0:T(8,128)S(1)}, f32[256,64]{1,0:T(8,128)}, u32[]{:S(2)}) copy-start(f32[256,64]{1,0:T(8,128)} %copy-done.22) | copy-start | bytes 196612
  322.8 7.9 %copy-start.19 = (bf16[256,6,128]{0,2,1:T(8,128)(2,1)}, bf16[256,6,128]{0,2,1:T(8,128)(2,1)S(1)}, u32[]{:S(2)}) copy-start(bf16[256,6,128]{0,2,1:T(8,128)(2,1)S(1)} %add_convert_fusion.3) | copy-start | bytes 1179652
  330.8 19.1 %copy-start.8 = (bf16[256,1536]{1,0:T(8,128)(2,1)S(1)}, bf16[256,1536]{1,0:T(8,128)(2,1)}, u32[]{:S(2)}) copy-start(bf16[256,1536]{1,0:T(8,128)(2,1)} %x_ref.1) | copy-start | bytes 2359300
  330.8 19.1 %copy-start.32 = (f32[256]{0:T(256)S(1)}, f32[256]{0:T(256)}, u32[]{:S(2)}) copy-start(f32[256]{0:T(256)} %copy-done.31) | copy-start | bytes 3076
  333.8 18.2 %copy-start.4 = (f32[256,1536]{1,0:T(8,128)S(1)}, f32[256,1536]{1,0:T(8,128)}, u32[]{:S(2)}) copy-start(f32[256,1536]{1,0:T(8,128)} %copy-done.3) | copy-start | bytes 4718596
  333.8 15.1 %collective-permute-start.6 = (bf16[256,1536]{1,0:T(8,128)(2,1)S(1)}, bf16[256,1536]{1,0:T(8,128)(2,1)S(1)}, u32[]{:S(2)}, u32[]{:S(2)}) collective-permute-start(bf16[256,1536]{1,0:T(8,128)(2,1)S(1)} %fusion.26), channel_id=1, source_target_pairs={{0,1},{1,0},{2,3},{3,2},{4,5},{5,4},{6,7},{7,6},{8,9},{9,8},{10,11... | collective-permute-start | bytes 2359304 | tf_op jit(solution)/shard_map/ppermute | solution.py:500
  349.0 0.9 copy-start.14
  351.3 99.8 %all-gather.10.cloned.1.call-start = ((), (), s32[]{:S(2)}) async-start(), calls=%async_computation.4 | async-start | bytes 3317760 | tf_op jit(solution)/shard_map/all_gather | solution.py:631
  352.0 189.2 %reduce-scatter.4.cloned.1.call-start = ((), (), s32[]{:S(2)}) async-start(), calls=%async_computation.5 | async-start | bytes 5849088
  367.0 0.7 copy-start.34
  367.0 217.8 %all-reduce.7.cloned.1.call-start = ((), (), s32[]{:S(2)}) async-start(), calls=%async_computation.2 | async-start | bytes 917504 | tf_op jit(solution)/shard_map/psum | solution.py:681
  543.2 47.7 %copy-start.1 = (bf16[4480,96]{0,1:T(8,128)(2,1)S(1)}, bf16[4480,96]{0,1:T(8,128)(2,1)}, u32[]{:S(2)}) copy-start(bf16[4480,96]{0,1:T(8,128)(2,1)} %param.29) | copy-start | bytes 2580484
Sparse Core Ops, SparseCore 0:
  55.4 99.2 all-gather.5
  351.4 65.6 all-gather.7
  418.8 32.2 all-gather.9
  455.1 86.1 reduce-scatter.3
  543.6 41.2 all-reduce.6

commit v3 on v2

--- a/solution.py
+++ b/solution.py
@@ -183,9 +183,24 @@
         self.started.append(copy)
         return copy
 
+    def sent(self, *copies):
+        for copy in copies:
+            copy.wait_send()
+            self.started = [other for other in self.started if other is not copy]
+
     def drain(self):
-        for copy in self.started:
-            copy.wait_send()
+        self.sent(*list(self.started))
+
+
+class Loads:
+    def __init__(self, sems):
+        self.sems, self.used = sems, 0
+
+    def start(self, src, dst):
+        copy = pltpu.make_async_copy(src, dst, self.sems.at[self.used])
+        self.used += 1
+        copy.start()
+        return copy
 
 
 def along_context():
@@ -201,14 +216,13 @@
 
 
 class RowSum:
-    def __init__(self, wire, part, out, from_prv, from_nxt, mine, other, chunks):
-        self.wire, self.part, self.out, self.chunks = wire, part, out, chunks
+    def __init__(self, wire, part, from_prv, from_nxt, mine, other, chunks):
+        self.wire, self.part, self.chunks = wire, part, chunks
         self.from_prv, self.from_nxt, self.mine, self.other = from_prv, from_nxt, mine, other
-        self.rows, self.width = out.shape
+        self.rows, self.width = mine.shape
         self.half = self.rows // 2
         self.c, self.nxt, self.prv, self.cf = along_context()
-        self.relay_p, self.relay_n, self.plain_p, self.plain_n = {}, {}, {}, {}
-        self.more_p, self.more_n, self.swap = {}, {}, {}
+        self.relays, self.plains, self.mores, self.swaps = {}, {}, {}, {}
 
     def cols(self, k):
         size = self.width // self.chunks
@@ -218,40 +232,48 @@
         at = pl.multiple_of(owner * self.rows + second * self.half, 16)
         return pl.ds(at, self.half), self.cols(k)
 
-    def start(self, k):
+    def start(self):
         up, down = {"context": self.nxt}, {"context": self.prv}
-        part, cols = self.part, self.cols(k)
-        push = self.wire.push
-        self.relay_p[k] = push(part.at[self.win(self.cf, 0, k)], self.from_prv.at[0, :, cols], up)
-        self.relay_n[k] = push(part.at[self.win(self.cf, 1, k)], self.from_nxt.at[0, :, cols], down)
-        self.plain_p[k] = push(part.at[self.win(self.nxt, 1, k)], self.from_prv.at[1, :, cols], up)
-        self.plain_n[k] = push(part.at[self.win(self.prv, 0, k)], self.from_nxt.at[1, :, cols], down)
+        part, push = self.part, self.wire.push
+        for k in range(self.chunks):
+            cols = self.cols(k)
+            self.relays[k] = (
+                push(part.at[self.win(self.cf, 0, k)], self.from_prv.at[0, :, cols], up),
+                push(part.at[self.win(self.cf, 1, k)], self.from_nxt.at[0, :, cols], down),
+            )
+        for k in range(self.chunks):
+            cols = self.cols(k)
+            self.plains[k] = (
+                push(part.at[self.win(self.nxt, 1, k)], self.from_prv.at[1, :, cols], up),
+                push(part.at[self.win(self.prv, 0, k)], self.from_nxt.at[1, :, cols], down),
+            )
 
     def relay(self, k):
         cols, push = self.cols(k), self.wire.push
-        self.relay_p[k].wait_recv()
+        self.relays[k][0].wait_recv()
         self.from_prv[0, :, cols] = (
             self.from_prv[0, :, cols].astype(f32) + self.part[self.win(self.nxt, 0, k)].astype(f32)
         ).astype(bf16)
-        self.more_p[k] = push(self.from_prv.at[0, :, cols], self.from_prv.at[2, :, cols], {"context": self.nxt})
-        self.relay_n[k].wait_recv()
+        one = push(self.from_prv.at[0, :, cols], self.from_prv.at[2, :, cols], {"context": self.nxt})
+        self.relays[k][1].wait_recv()
         self.from_nxt[0, :, cols] = (
             self.from_nxt[0, :, cols].astype(f32) + self.part[self.win(self.prv, 1, k)].astype(f32)
         ).astype(bf16)
-        self.more_n[k] = push(self.from_nxt.at[0, :, cols], self.from_nxt.at[2, :, cols], {"context": self.prv})
+        two = push(self.from_nxt.at[0, :, cols], self.from_nxt.at[2, :, cols], {"context": self.prv})
+        self.mores[k] = (one, two)
 
     def exchange(self, k):
         cols, half = self.cols(k), self.half
-        self.plain_n[k].wait_recv()
-        self.more_p[k].wait_recv()
+        self.plains[k][1].wait_recv()
+        self.mores[k][0].wait_recv()
         first = (
             self.part[self.win(self.c, 0, k)].astype(f32)
             + self.from_nxt[1, :, cols].astype(f32)
             + self.from_prv[2, :, cols].astype(f32)
         )
         self.mine[pl.ds(0, half), cols] = first.astype(bf16)
-        self.plain_p[k].wait_recv()
-        self.more_n[k].wait_recv()
+        self.plains[k][0].wait_recv()
+        self.mores[k][1].wait_recv()
         second = (
             self.part[self.win(self.c, 1, k)].astype(f32)
             + self.from_prv[1, :, cols].astype(f32)
@@ -259,82 +281,105 @@
         )
         self.mine[pl.ds(half, half), cols] = second.astype(bf16)
         to = {"tensor": 1 - lax.axis_index("tensor")}
-        self.swap[k] = self.wire.push(self.mine.at[:, cols], self.other.at[:, cols], to)
-
-    def finish(self, k):
-        cols = self.cols(k)
-        self.swap[k].wait_recv()
-        total = self.mine[:, cols].astype(f32) + self.other[:, cols].astype(f32)
-        self.out[:, cols] = total.astype(self.out.dtype)
+        self.swaps[k] = self.wire.push(self.mine.at[:, cols], self.other.at[:, cols], to)
+
+    def landed(self):
+        for k in range(self.chunks):
+            self.swaps[k].wait_recv()
+
+    def total(self, rows):
+        return self.mine[rows, :].astype(f32) + self.other[rows, :].astype(f32)
 
 
 class ShardSum:
-    def __init__(self, wire, got, from_down, from_up, pair, last, chunks):
-        self.wire, self.got, self.from_down, self.from_up = wire, got, from_down, from_up
-        self.pair, self.last, self.chunks = pair, last, chunks
-        self.shard, width = got.shape[1:]
-        self.half, self.size = self.shard // 2, width // chunks
+    def __init__(self, wire, both, came, from_down, from_up, pair, last, ranges):
+        self.wire, self.both, self.came = wire, both, came
+        self.from_down, self.from_up = from_down, from_up
+        self.pair, self.last, self.ranges = pair, last, ranges
+        self.shard = both.shape[2]
+        self.half = self.shard // 2
         self.f, self.core, self.far, self.up, self.down = along_fsdp()
         self.side = lax.rem(lax.div(self.f, 2), 2)
         self.mine = lax.rem(self.f, 2)
+        self.z = lax.div(self.f, 4)
         self.cores, self.plain, self.relay, self.more, self.cross = {}, {}, {}, {}, {}
 
     def cols(self, k):
-        return pl.ds(k * self.size, self.size)
-
-    def send_core(self, k, rel, src):
+        return pl.ds(*self.ranges[k])
+
+    def block_cols(self, rel):
+        size = 4 * self.shard
+        return pl.ds(pl.multiple_of(lax.rem(self.z + rel, 4) * size, 128), size)
+
+    def multiply(self, k, rel, left, right):
+        tile = lax.dot_general(
+            left, right, (((0,), (0,)), ((), ())), preferred_element_type=f32
+        ).astype(bf16)
+        cols = self.cols(k)
+        for side in range(2):
+            for core in range(2):
+                lo = (2 * side + core) * self.shard
+                place = lax.rem(core + self.mine, 2)
+                self.both[place, 2 * rel + side, :, cols] = tile[lo : lo + self.shard]
         self.cores[k, rel] = self.wire.push(
-            src, self.got.at[pl.ds(2 * rel, 2), :, self.cols(k)], {"fsdp": self.core}
+            self.both.at[1, pl.ds(2 * rel, 2), :, cols],
+            self.came.at[pl.ds(2 * rel, 2), :, cols],
+            {"fsdp": self.core},
         )
 
-    def add_core(self, k, rel, own):
+    def block(self, rel, second, k):
+        return pl.ds(2 * rel, 2), pl.ds(second * self.half, self.half), self.cols(k)
+
+    def add_core(self, k, rel):
         self.cores[k, rel].wait_recv()
         at = pl.ds(2 * rel, 2), slice(None), self.cols(k)
-        self.got[at] = (self.got[at].astype(f32) + own.astype(f32)).astype(bf16)
-
-    def block(self, rel, second, k):
-        return pl.ds(2 * rel, 2), pl.ds(second * self.half, self.half), self.cols(k)
+        mine = (0,) + at
+        self.both[mine] = (self.both[mine].astype(f32) + self.came[at].astype(f32)).astype(bf16)
 
     def start(self, k):
-        got, cols, push = self.got, self.cols(k), self.wire.push
+        got, cols, push = self.both.at[0], self.cols(k), self.wire.push
         up, down = {"fsdp": self.up}, {"fsdp": self.down}
+        self.add_core(k, 2)
         self.relay[k] = (
             push(got.at[self.block(2, 0, k)], self.from_down.at[0, :, :, cols], up),
             push(got.at[self.block(2, 1, k)], self.from_up.at[0, :, :, cols], down),
         )
+        self.add_core(k, 1)
+        self.add_core(k, 3)
         self.plain[k] = (
             push(got.at[self.block(1, 1, k)], self.from_down.at[1, :, :, cols], up),
             push(got.at[self.block(3, 0, k)], self.from_up.at[1, :, :, cols], down),
         )
+        self.add_core(k, 0)
 
     def relays(self, k):
-        cols, push = self.cols(k), self.wire.push
+        got, cols, push = self.both.at[0], self.cols(k), self.wire.push
         self.relay[k][0].wait_recv()
         at = (0, slice(None), slice(None), cols)
         self.from_down[at] = (
-            self.from_down[at].astype(f32) + self.got[self.block(1, 0, k)].astype(f32)
+            self.from_down[at].astype(f32) + got[self.block(1, 0, k)].astype(f32)
         ).astype(bf16)
         one = push(self.from_down.at[at], self.from_down.at[2, :, :, cols], {"fsdp": self.up})
         self.relay[k][1].wait_recv()
         self.from_up[at] = (
-            self.from_up[at].astype(f32) + self.got[self.block(3, 1, k)].astype(f32)
+            self.from_up[at].astype(f32) + got[self.block(3, 1, k)].astype(f32)
         ).astype(bf16)
         two = push(self.from_up.at[at], self.from_up.at[2, :, :, cols], {"fsdp": self.down})
         self.more[k] = (one, two)
 
     def across(self, k):
-        cols, half = self.cols(k), self.half
+        got, cols, half = self.both.at[0], self.cols(k), self.half
         self.more[k][0].wait_recv()
         self.plain[k][1].wait_recv()
         self.pair[:, pl.ds(0, half), cols] = (
-            self.got[self.block(0, 0, k)].astype(f32)
+            got[self.block(0, 0, k)].astype(f32)
             + self.from_down[2, :, :, cols].astype(f32)
             + self.from_up[1, :, :, cols].astype(f32)
         ).astype(bf16)
         self.more[k][1].wait_recv()
         self.plain[k][0].wait_recv()
         self.pair[:, pl.ds(half, half), cols] = (
-            self.got[self.block(0, 1, k)].astype(f32)
+            got[self.block(0, 1, k)].astype(f32)
             + self.from_down[1, :, :, cols].astype(f32)
             + self.from_up[2, :, :, cols].astype(f32)
         ).astype(bf16)
@@ -348,16 +393,6 @@
         return self.pair[self.side, :, cols].astype(f32) + self.last[:, cols].astype(f32)
 
 
-def shard_scratch(shard, width, blocks=8):
-    return [
-        pltpu.VMEM((blocks, shard, width), bf16),
-        pltpu.VMEM((3, 2, shard // 2, width), bf16),
-        pltpu.VMEM((3, 2, shard // 2, width), bf16),
-        pltpu.VMEM((2, shard, width), bf16),
-        pltpu.VMEM((shard, width), bf16),
-    ]
-
-
 def row_scratch(rows, width):
     return [pltpu.VMEM((3, rows // 2, width), bf16)] * 2 + [pltpu.VMEM((rows, width), bf16)] * 2
 
@@ -370,86 +405,359 @@
     ]
 
 
+def half_turn(x):
+    return pltpu.roll(x, HD // 2, 1)
+
+
+def signal(sem, to):
+    pl.semaphore_signal(sem, inc=1, device_id=to, device_id_type=MESH)
+
+
 ORDER = (2, 1, 3, 0)
-
-
-def mlp_back_kernel(
-    normed_ref, dy_ref, gate_ref, lift_ref, hidden_ref, first_ref, second_ref,
-    first_out, second_out, shard_out,
-    grads, got, from_down, from_up, pair, last,
-    prv1, nxt1, mine1, other1, prv2, nxt2, mine2, other2, send, recv,
+SMALL = (8, 512)
+
+
+def layer_back_kernel(
+    normed_hbm, dy_hbm, gate_hbm, lift_hbm, hidden_hbm, first_hbm, second_hbm,
+    out_hbm, lin_hbm, probs_hbm,
+    middle_ref, dy_ref, gain_two_ref, mixed_ref, query_ref, key_ref, value_ref,
+    normed_one_ref, tokens_ref, gain_one_ref, cos_ref, sin_ref,
+    result_ref, gt_ref, small_ref, attn_ref, mlp_hbm,
+    part, from_prv, from_nxt, mine, other,
+    left, right, both, came, from_down, from_up, pair, last, shard_out,
+    probs, d_middle, d_branch, d_mixed, acc_k, acc_v, kv_send, kv_came,
+    d_lin, swap_mine, swap_other, attn_own, attn_came, small_own, small_came,
+    send, recv, local, free,
 ):
-    wire = Wire(send, recv)
-    meet(everyone_near())
-    chunks = 3
-    sums = ShardSum(wire, got, from_down, from_up, pair, last, chunks)
-    rows1 = RowSum(wire, first_ref, first_out, prv1, nxt1, mine1, other1, chunks)
-    rows2 = RowSum(wire, second_ref, second_out, prv2, nxt2, mine2, other2, chunks)
-    shard, span = sums.shard, sums.size
-    z = lax.div(sums.f, 4)
-    for k in range(chunks):
-        rows1.start(k)
-    pairs = ((normed_ref, gate_ref), (normed_ref, lift_ref), (dy_ref, hidden_ref))
-    for k, (left, right) in enumerate(pairs):
-        for rel in ORDER:
-            at = pl.multiple_of(lax.rem(z + rel, 4) * (4 * shard), 4 * shard)
-            tile = jnp.dot(left[pl.ds(at, 4 * shard), :], right[...], preferred_element_type=f32).astype(bf16)
-            for side in range(2):
-                for core in range(2):
-                    lo = (2 * side + core) * shard
-                    grads[core, 2 * rel + side, :, sums.cols(k)] = tile[lo : lo + shard]
-            sums.send_core(k, rel, grads.at[1 - sums.mine, pl.ds(2 * rel, 2), :, sums.cols(k)])
+    wire, loads = Wire(send, recv), Loads(local)
+    rows, width = middle_ref.shape
+    group = part.shape[0]
+    q_cols, kv_cols = mixed_ref.shape[1], key_ref.shape[1]
+    heads = q_cols // HD
+    span = hidden_hbm.shape[1]
+    scale = HD ** (-0.5)
+    c, nxt, prv, cf = along_context()
+    f, core, far, up, down = along_fsdp()
+    C = lambda i: {"context": i}
+    F = lambda i: {"fsdp": i}
+    T = {"tensor": 1 - lax.axis_index("tensor")}
+
+    def keep_small(at, values):
+        for k in range(values.shape[1] // SMALL[1]):
+            small_own[pl.ds(at + k, 1), :] = values[:, k * SMALL[1] : (k + 1) * SMALL[1]]
+
+    load_part = loads.start(first_hbm, part)
+    load_left = loads.start(normed_hbm, left)
+    load_r0 = loads.start(gate_hbm, right.at[0])
+    load_r1 = loads.start(lift_hbm, right.at[1])
+    opposite = lax.rem(f + 8, lax.axis_size("fsdp"))
+    meet(everyone_near() + [C(cf), F(opposite)])
+
+    one = RowSum(wire, part, from_prv, from_nxt, mine, other, 3)
+    two = RowSum(wire, part, from_prv, from_nxt, mine, other, 3)
+    mlp = ShardSum(wire, both, came, from_down, from_up, pair, last, [(k * span, span) for k in range(3)])
+    attn = ShardSum(
+        wire, both, came, from_down, from_up, pair, last,
+        [(0, q_cols), (q_cols, q_cols), (2 * q_cols, 2 * kv_cols)],
+    )
+    load_part.wait()
+    one.start()
+
+    load_left.wait()
+    load_r0.wait()
+    for rel in ORDER:
+        mlp.multiply(0, rel, left[:, mlp.block_cols(rel)], right[0])
+    load_r0 = loads.start(hidden_hbm, right.at[0])
+    load_r1.wait()
+    for rel in ORDER:
+        mlp.multiply(1, rel, left[:, mlp.block_cols(rel)], right[1])
+    load_left = loads.start(dy_hbm, left)
+    for k in range(3):
+        one.relay(k)
+    mlp.start(0)
+    load_r0.wait()
+    load_left.wait()
+    for rel in ORDER:
+        mlp.multiply(2, rel, left[:, mlp.block_cols(rel)], right[0])
+    deep = left.shape[0]
+    rest = width - deep
+    load_out = (
+        loads.start(out_hbm.at[pl.ds(0, deep)], left.at[:, pl.ds(0, q_cols)]),
+        loads.start(out_hbm.at[pl.ds(deep, rest)], left.at[pl.ds(0, rest), pl.ds(q_cols, q_cols)]),
+    )
+    lin_cols = lin_hbm.shape[1]
+    load_lin = (
+        loads.start(lin_hbm.at[pl.ds(0, deep)], right.at[0, :, pl.ds(0, lin_cols)]),
+        loads.start(lin_hbm.at[pl.ds(deep, rest)], right.at[1, pl.ds(0, rest), pl.ds(0, lin_cols)]),
+    )
+    load_probs = {h: loads.start(probs_hbm.at[h], probs.at[h % 2]) for h in range(2)}
+    mlp.start(1)
+    one.exchange(0)
+    one.exchange(1)
+    mlp.start(2)
+    one.exchange(2)
+    signal(free.at[0], F(core))
+    for k in range(3):
+        wire.sent(*one.relays[k], *one.plains[k], *one.mores[k])
+    signal(free.at[1], C(nxt))
+    signal(free.at[2], C(prv))
+    load_part = loads.start(second_hbm, part)
+    mlp.relays(0)
+    mlp.relays(1)
+    one.landed()
+
+    sizes = 64
+    gain_grad = jnp.zeros((1, width), f32)
+    for at in range(0, rows, sizes):
+        at = pl.ds(at, sizes)
+        grad, mid = one.total(at), middle_ref[at, :]
+        r = lax.rsqrt(jnp.mean(mid * mid, axis=-1, keepdims=True) + EPSILON)
+        gain_grad += jnp.sum(grad * mid * r, axis=0, keepdims=True)
+        scaled = grad * gain_two_ref[...]
+        back = jnp.mean(scaled * mid, axis=-1, keepdims=True)
+        value = dy_ref[at, :].astype(f32) + r * scaled - mid * (r * r * r * back)
+        d_middle[at, :] = value
+        d_branch[at, :] = value.astype(bf16)
+    keep_small(3, gain_grad)
+    wire.sent(*one.swaps.values())
+    signal(free.at[3], T)
+    load_part.wait()
+    pl.semaphore_wait(free.at[1], 1)
+    pl.semaphore_wait(free.at[2], 1)
+    two.start()
+    mlp.relays(2)
+
+    for copy in load_out:
+        copy.wait()
+    d_mixed[...] = (
+        jnp.dot(d_branch[:, pl.ds(0, deep)], left[:, pl.ds(0, q_cols)], preferred_element_type=f32)
+        + jnp.dot(
+            d_branch[:, pl.ds(deep, rest)], left[pl.ds(0, rest), pl.ds(q_cols, q_cols)],
+            preferred_element_type=f32,
+        )
+    ).astype(bf16)
+    lane = lax.broadcasted_iota(jnp.int32, (1, HD), 1)
+    sign = jnp.where(lane < HD // 2, 1.0, -1.0).astype(f32)
+
+    def turn_back(w):
+        return w * cos_ref[...] + half_turn(w * sin_ref[...]) * sign
+
+    nt = (((1,), (1,)), ((), ()))
+    tn = (((0,), (0,)), ((), ()))
+
+    def head(h):
+        cols = pl.ds(h * HD, HD)
+        load_probs[h].wait()
+        p = probs[h % 2]
+        dm = d_mixed[:, cols]
+        dp = lax.dot_general(dm, value_ref[...], nt, preferred_element_type=f32)
+        inner = jnp.sum(p * dp, axis=-1, keepdims=True)
+        ds = (p * (dp - inner)).astype(bf16)
+        dq = jnp.dot(ds, key_ref[...], preferred_element_type=f32) * scale
+        d_lin[:, cols] = turn_back(dq).astype(bf16)
+        dk = lax.dot_general(ds, query_ref[:, cols], tn, preferred_element_type=f32)
+        dv = lax.dot_general(p.astype(bf16), dm, tn, preferred_element_type=f32)
+        if h == 0:
+            acc_k[...] = dk
+            acc_v[...] = dv
+        else:
+            acc_k[...] += dk
+            acc_v[...] += dv
+        if h + 2 < heads:
+            load_probs[h + 2] = loads.start(probs_hbm.at[h + 2], probs.at[h % 2])
+
+    head(0)
+    mlp.across(0)
+    head(1)
+    mlp.across(1)
+    for k in range(3):
+        two.relay(k)
+    head(2)
+    mlp.across(2)
+    for k in range(3):
+        wire.sent(*mlp.more[k])
+    signal(free.at[4], F(up))
+    signal(free.at[5], F(down))
+    head(3)
+    for k in range(3):
+        shard_out[:, mlp.cols(k)] = mlp.total(k).astype(bf16)
+    signal(free.at[6], F(far))
+    spread = [
+        wire.push(shard_out, mlp_hbm.at[c], C(nxt)),
+        wire.push(shard_out, mlp_hbm.at[c], C(prv)),
+    ]
+    keep = loads.start(shard_out, mlp_hbm.at[c])
+    head(4)
+    pl.semaphore_wait(free.at[3], 1)
+    for k in range(3):
+        two.exchange(k)
+    head(5)
+
+    for k in range(4):
+        kv_send[k, 0] = acc_k[pl.ds(k * rows, rows), :].astype(bf16)
+        kv_send[k, 1] = acc_v[pl.ds(k * rows, rows), :].astype(bf16)
+    kv = [
+        wire.push(kv_send.at[nxt], kv_came.at[0], C(nxt)),
+        wire.push(kv_send.at[prv], kv_came.at[1], C(prv)),
+        wire.push(kv_send.at[cf], kv_came.at[2], C(cf)),
+    ]
+    for k in range(3):
+        wire.sent(*[mlp.cores[k, rel] for rel in ORDER], *mlp.relay[k], *mlp.plain[k], mlp.cross[k])
+    pl.semaphore_wait(free.at[0], 1)
+    for rel in ORDER:
+        attn.multiply(0, rel, d_branch[:, attn.block_cols(rel)], mixed_ref[...])
+    for rel in ORDER:
+        attn.multiply(1, rel, normed_one_ref[:, attn.block_cols(rel)], d_lin[:, pl.ds(0, q_cols)])
+    for copy in kv:
+        copy.wait_recv()
+    d_key = acc_k[pl.ds(pl.multiple_of(c * rows, 8), rows), :]
+    d_value = acc_v[pl.ds(pl.multiple_of(c * rows, 8), rows), :]
+    for k in range(3):
+        d_key += kv_came[k, 0].astype(f32)
+        d_value += kv_came[k, 1].astype(f32)
+    d_lin[:, pl.ds(q_cols, kv_cols)] = turn_back(d_key * scale).astype(bf16)
+    d_lin[:, pl.ds(q_cols + kv_cols, kv_cols)] = d_value.astype(bf16)
+    for copy in load_lin:
+        copy.wait()
+    swap_mine[:, pl.ds(0, deep)] = lax.dot_general(
+        d_lin[...], right[0, :, pl.ds(0, lin_cols)], nt, preferred_element_type=f32
+    ).astype(bf16)
+    swap_mine[:, pl.ds(deep, rest)] = lax.dot_general(
+        d_lin[...], right[1, pl.ds(0, rest), pl.ds(0, lin_cols)], nt, preferred_element_type=f32
+    ).astype(bf16)
+    swap = wire.push(swap_mine, swap_other, T)
+    for rel in ORDER:
+        attn.multiply(
+            2, rel, normed_one_ref[:, attn.block_cols(rel)], d_lin[:, pl.ds(q_cols, 2 * kv_cols)]
+        )
+    pl.semaphore_wait(free.at[4], 1)
+    pl.semaphore_wait(free.at[5], 1)
+    for k in range(3):
+        attn.start(k)
+    keep_small(6, jnp.sum(d_lin[...].astype(f32), axis=0, keepdims=True))
+    half = shard_out.shape[0] // 2
+    spread[0].wait_recv()
+    w = mlp_hbm.at[prv, pl.ds(0, half)]
+    spread.append(wire.push(w, w, C(nxt)))
+    spread[1].wait_recv()
+    w = mlp_hbm.at[nxt, pl.ds(half, half)]
+    spread.append(wire.push(w, w, C(prv)))
+    two.landed()
+    for at in range(0, rows, sizes):
+        at = pl.ds(at, sizes)
+        result_ref[at, :] = (middle_ref[at, :] + two.total(at)).astype(bf16)
+    for k in range(3):
+        attn.relays(k)
+    pl.semaphore_wait(free.at[6], 1)
+    for k in range(3):
+        attn.across(k)
+
+    swap.wait_recv()
+    gain_grad = jnp.zeros((1, width), f32)
+    for at in range(0, rows, sizes):
+        at = pl.ds(at, sizes)
+        grad = swap_mine[at, :].astype(f32) + swap_other[at, :].astype(f32)
+        mid = tokens_ref[at, :].astype(f32)
+        r = lax.rsqrt(jnp.mean(mid * mid, axis=-1, keepdims=True) + EPSILON)
+        gain_grad += jnp.sum(grad * mid * r, axis=0, keepdims=True)
+        scaled = grad * gain_one_ref[...]
+        back = jnp.mean(scaled * mid, axis=-1, keepdims=True)
+        gt_ref[at, :] = d_middle[at, :] + r * scaled - mid * (r * r * r * back)
+    keep_small(0, gain_grad)
+
+    for k in range(3):
+        attn_own[:, attn.cols(k)] = attn.total(k).astype(bf16)
+    both_ways = [
+        wire.push(attn_own, attn_came.at[0], C(nxt)),
+        wire.push(attn_own, attn_came.at[1], C(prv)),
+    ]
+    steps = [F(core), F(far), F(f + 4 - 8 * lax.rem(lax.div(f, 4), 2)), F(opposite),
+             C(c + 1 - 2 * lax.rem(c, 2)), C(cf)]
+    for k, to in enumerate(steps):
+        copy = wire.push(small_own if k == 0 else small_came.at[2 * k - 1], small_came.at[2 * k], to)
+        copy.wait_recv()
+        have = small_own[...] if k == 0 else small_came[2 * k - 1]
+        total = have + small_came[2 * k]
+        if k == len(steps) - 1:
+            small_ref[...] = total
+        else:
+            small_came[2 * k + 1] = total
         if k == 1:
-            for j in range(chunks):
-                rows1.relay(j)
-            for j in range(chunks):
-                rows2.start(j)
-        if k >= 1:
-            for rel in ORDER:
-                sums.add_core(k - 1, rel, grads[sums.mine, pl.ds(2 * rel, 2), :, sums.cols(k - 1)])
-            sums.start(k - 1)
-    for rel in ORDER:
-        sums.add_core(2, rel, grads[sums.mine, pl.ds(2 * rel, 2), :, sums.cols(2)])
-    sums.start(2)
-    for k in range(chunks):
-        rows1.exchange(k)
-        sums.relays(k)
-    for k in range(chunks):
-        rows2.relay(k)
-    for k in range(chunks):
-        rows1.finish(k)
-        sums.across(k)
-    for k in range(chunks):
-        rows2.exchange(k)
-    for k in range(chunks):
-        shard_out[:, sums.cols(k)] = sums.total(k).astype(bf16)
-        rows2.finish(k)
+            both_ways[0].wait_recv()
+            both_ways[1].wait_recv()
+            both_ways.append(
+                wire.push(attn_came.at[0, pl.ds(0, half)], attn_came.at[2, pl.ds(0, half)], C(nxt))
+            )
+            both_ways.append(
+                wire.push(attn_came.at[1, pl.ds(half, half)], attn_came.at[2, pl.ds(half, half)], C(prv))
+            )
+    both_ways[2].wait_recv()
+    both_ways[3].wait_recv()
+    own_pair = attn_own[...].astype(f32) + attn_came[2].astype(f32)
+    next_pair = attn_came[0].astype(f32) + attn_came[1].astype(f32)
+    attn_ref[...] = own_pair + next_pair
+    spread[2].wait_recv()
+    spread[3].wait_recv()
+    keep.wait()
     wire.drain()
 
 
-def mlp_back(normed_turned, dy_turned, d_gate, d_lift, hidden, first, second, cid=3):
-    width = normed_turned.shape[0]
-    rows, span = first.shape[0] // 4, d_gate.shape[1]
-    shard = width // 16
-    sems = 3 * (4 + 4 + 2 + 1) + 2 * 3 * 7
+def layer_back(hbm, near, cid=4):
+    normed, dy, gate, lift, hidden, first, second, out, lin, probs = hbm
+    group, width = normed.shape
+    rows = group // 4
+    shard, span = width // 16, gate.shape[1]
+    lin_cols = lin.shape[1]
+    q_cols = out.shape[1]
+    sems = 2 * 21 + 2 * (12 + 3 * 7) + 3 + 1 + 4 + 4 + 6
     return pl.pallas_call(
-        mlp_back_kernel,
+        layer_back_kernel,
         out_shape=(
+            jax.ShapeDtypeStruct((rows, width), bf16),
             jax.ShapeDtypeStruct((rows, width), f32),
-            jax.ShapeDtypeStruct((rows, width), bf16),
-            jax.ShapeDtypeStruct((shard, 3 * span), bf16),
+            jax.ShapeDtypeStruct(SMALL, f32),
+            jax.ShapeDtypeStruct((shard, lin_cols + q_cols), f32),
+            jax.ShapeDtypeStruct((4, shard, 3 * span), bf16),
         ),
-        in_specs=[VM] * 7,
-        out_specs=(VM,) * 3,
-        scratch_shapes=[pltpu.VMEM((2, 8, shard, 3 * span), bf16)]
-        + shard_scratch(shard, 3 * span)
-        + row_scratch(rows, width) * 2
-        + [pltpu.SemaphoreType.DMA((sems,)), pltpu.SemaphoreType.DMA((sems,))],
+        in_specs=[ANY] * len(hbm) + [VM] * len(near),
+        out_specs=(VM, VM, VM, VM, ANY),
+        scratch_shapes=[pltpu.VMEM((group, width), bf16)]
+        + row_scratch(rows, width)
+        + [
+            pltpu.VMEM((group, width), bf16),
+            pltpu.VMEM((2, group, span), bf16),
+            pltpu.VMEM((2, 8, shard, 3 * span), bf16),
+            pltpu.VMEM((8, shard, 3 * span), bf16),
+            pltpu.VMEM((3, 2, shard // 2, 3 * span), bf16),
+            pltpu.VMEM((3, 2, shard // 2, 3 * span), bf16),
+            pltpu.VMEM((2, shard, 3 * span), bf16),
+            pltpu.VMEM((shard, 3 * span), bf16),
+            pltpu.VMEM((shard, 3 * span), bf16),
+            pltpu.VMEM((2, rows, group), f32),
+            pltpu.VMEM((rows, width), f32),
+            pltpu.VMEM((rows, width), bf16),
+            pltpu.VMEM((rows, q_cols), bf16),
+            pltpu.VMEM((group, HD), f32),
+            pltpu.VMEM((group, HD), f32),
+            pltpu.VMEM((4, 2, rows, HD), bf16),
+            pltpu.VMEM((3, 2, rows, HD), bf16),
+            pltpu.VMEM((rows, lin_cols), bf16),
+            pltpu.VMEM((rows, width), bf16),
+            pltpu.VMEM((rows, width), bf16),
+            pltpu.VMEM((shard, lin_cols + q_cols), bf16),
+            pltpu.VMEM((3, shard, lin_cols + q_cols), bf16),
+            pltpu.VMEM(SMALL, f32),
+            pltpu.VMEM((11,) + SMALL, f32),
+            pltpu.SemaphoreType.DMA((sems,)),
+            pltpu.SemaphoreType.DMA((sems,)),
+            pltpu.SemaphoreType.DMA((18,)),
+            pltpu.SemaphoreType.REGULAR((7,)),
+        ],
         compiler_params=pltpu.CompilerParams(
-            collective_id=cid, has_side_effects=True, vmem_limit_bytes=62 << 20
+            collective_id=cid, has_side_effects=True, vmem_limit_bytes=63 << 20
         ),
-        name="mlp_back",
-    )(normed_turned, dy_turned, d_gate, d_lift, hidden, first, second)
+        name="layer_back",
+    )(*hbm, *near)
 
 
 def rms_norm(values, gain_vec):
@@ -495,12 +803,6 @@
     )
 
 
-def swap_sum(x, axis):
-    low = x.astype(jnp.bfloat16)
-    other = lax.ppermute(low, axis, [(0, 1), (1, 0)])
-    return low.astype(jnp.float32) + other.astype(jnp.float32)
-
-
 def around(x):
     size, rank = lax.axis_size("context"), lax.axis_index("context")
     parts = [x] + [
@@ -509,16 +811,6 @@
     twice = jnp.concatenate(parts + parts, axis=0)
     rows = x.shape[0]
     return lax.dynamic_slice_in_dim(twice, (size - rank) % size * rows, size * rows)
-
-
-def back_around(x):
-    size, rank = lax.axis_size("context"), lax.axis_index("context")
-    rows = x.shape[0] // size
-    total = lax.dynamic_slice_in_dim(x, rank * rows, rows)
-    for k in range(1, size):
-        block = lax.dynamic_slice_in_dim(x, (rank + k) % size * rows, rows)
-        total = total + lax.ppermute(block, "context", [(i, (i + k) % size) for i in range(size)])
-    return total
 
 
 def hidden_range(width, parts, rank):
@@ -624,86 +916,40 @@
     d_lift = jnp.where(keep, d_hidden * swish, 0.0).astype(bf16)
     d_normed_part = tail_dot(d_gate, gate_full) + tail_dot(d_lift, lift_full)
     mlp_part = tail_dot(hidden, down_turned).astype(bf16)
-    d_normed_two, mlp_branch, mlp_shard = mlp_back(
-        normed_group.T, dy_group.T, d_gate, d_lift, hidden, d_normed_part.astype(bf16), mlp_part
-    )
-    result = (middle + mlp_branch.astype(f32)).astype(bf16)
-    mlp_all = lax.all_gather(mlp_shard, "context", axis=0)
+    result, grad_tokens, small, attn_shard, mlp_all = layer_back(
+        (
+            normed_group, dy_group, d_gate, d_lift, hidden, d_normed_part.astype(bf16), mlp_part,
+            out_turned, lin_full, probs.reshape(heads_query, row_count, group_rows),
+        ),
+        (
+            middle, cotangent, gain_two[None], mixed, query_heads.reshape(row_count, query_cols),
+            key_group.reshape(group_rows, kv_cols), value_group.reshape(group_rows, kv_cols),
+            normed_one, tokens, gain_one[None], cosine, sine_table,
+        ),
+    )
 
     def whole(k):
         parts = [mlp_all[i, :, k * span : (k + 1) * span] for i in range(context_size)]
         parts[-1] = parts[-1][:, overlap:]
         return jnp.concatenate(parts, axis=1).astype(f32)
 
-    _, pull_two = jax.vjp(rms_norm, middle, gain_two)
-    d_middle_norm, grad_gain_mlp = pull_two(d_normed_two)
-    d_middle = cotangent.astype(f32) + d_middle_norm
-    d_branch = d_middle.astype(bf16)
-    grad_w_out = lead_dot(d_branch, mixed)
-    d_mixed = (
-        jnp.dot(d_branch, out_turned, preferred_element_type=f32)
-        .astype(bf16)
-        .reshape(row_count, heads_kv, per_group, HD)
-    )
-    d_probs = jnp.einsum("qgjd,kgd->gjqk", d_mixed, value_group, preferred_element_type=f32)
-    inner = jnp.sum(probs * d_probs, axis=-1, keepdims=True)
-    d_scores = (probs * (d_probs - inner)).astype(bf16)
-    d_query = (
-        jnp.einsum("gjqk,kgd->qgjd", d_scores, key_group, preferred_element_type=f32) * score_scale
-    )
-    d_key_part = (
-        jnp.einsum("gjqk,qgjd->kgd", d_scores, query_heads, preferred_element_type=f32)
-        * score_scale
-    )
-    d_value_part = jnp.einsum("gjqk,qgjd->kgd", probs_low, d_mixed, preferred_element_type=f32)
-    d_kv = back_around(jnp.concatenate([d_key_part, d_value_part], axis=1))
-    d_key, d_value = d_kv[:, :heads_kv], d_kv[:, heads_kv:]
-
-    def turn_query(values):
-        return rotate(values, cosine, sine_table)
-
-    _, pull_query = jax.vjp(turn_query, query_lin.reshape(row_count, heads_query, HD))
-    _, pull_key = jax.vjp(turn_query, key_lin.reshape(row_count, heads_kv, HD))
-    d_query_lin = pull_query(d_query.reshape(row_count, heads_query, HD))[0]
-    d_key_lin = pull_key(d_key)[0]
-    d_lin = jnp.concatenate(
-        [
-            d_query_lin.reshape(row_count, query_cols),
-            d_key_lin.reshape(row_count, kv_cols),
-            d_value.reshape(row_count, kv_cols),
-        ],
-        axis=1,
-    ).astype(bf16)
-    bias_part = jnp.sum(d_lin.astype(f32), axis=0)
-    attn_grads = jnp.concatenate(
-        [lead_dot(normed_one, d_lin).astype(bf16), grad_w_out.astype(bf16)], axis=1
-    )
-    attn_shard = lax.psum(
-        lax.psum_scatter(attn_grads, "fsdp", scatter_dimension=0, tiled=True), "context"
-    ).astype(f32)
-    d_normed_one = swap_sum(tail_dot(d_lin, lin_full), "tensor")
-    _, pull_one = jax.vjp(rms_norm, inputs, gain_one)
-    d_input_norm, grad_gain_attn = pull_one(d_normed_one)
-    grad_tokens = d_middle + d_input_norm
-    small = jnp.sum(
-        lax.all_gather(
-            jnp.concatenate([grad_gain_attn, grad_gain_mlp, bias_part])[None], ("fsdp", "context"), axis=0, tiled=True
-        ),
-        axis=0,
-    )
+    small = small.reshape(-1)
     own = lambda at: lax.dynamic_slice_in_dim(small, at + fsdp_rank * shard, shard)
     bias_total = small[2 * width :]
+    at_query = query_cols
+    at_key = at_query + query_cols
+    at_value = at_key + kv_cols
     return (
         result,
         grad_tokens,
         own(0),
-        attn_shard[:, :query_cols],
+        attn_shard[:, at_query:at_key],
         bias_total[:query_cols],
-        attn_shard[:, query_cols : query_cols + kv_cols],
+        attn_shard[:, at_key:at_value],
         bias_total[query_cols : query_cols + kv_cols],
-        attn_shard[:, query_cols + kv_cols : lin_cols],
+        attn_shard[:, at_value:],
         bias_total[query_cols + kv_cols :],
-        attn_shard[:, lin_cols:].T,
+        attn_shard[:, :query_cols].T,
         own(width),
         whole(0),
         whole(1),

time: 604 us -> 375 us (0.62)
  waiting for transfers between devices: 225 us -> 1.4 us
  Pallas kernels: 188 us -> 242 us
  local copies, waits for them, and re-layouts: 55.3 us -> 33.6 us
  matrix products: 71.5 us -> 52.7 us
  other arithmetic: 32.1 us -> 18.3 us
  starting transfers between devices: 11 us -> 4.65 us
    unnamed x6 -> x1, waiting for transfers between devices: 86.2 us -> 0.02 us
    all_gather x2 -> x0, waiting for transfers between devices: 77.3 us -> none  [the longest x1 46.6 us: on_device(): lax.all_gather(jnp.concatenate([grad_gain_attn, grad_gain_mlp, bias_part]...]
    pallas_call x1, Pallas kernels: 94.7 us -> 150 us  [layer_back(): pl.pallas_call(layer_back_kernel, out_shape=(jax.ShapeDtypeStruct((rows,...]
    psum x1 -> x0, waiting for transfers between devices: 40.3 us -> none  [on_device(): lax.psum(lax.psum_scatter(attn_grads, 'fsdp', scatter_dimension=0, tiled=...]
    ppermute x4 -> x0, waiting for transfers between devices: 21 us -> none  [the longest x1 13.7 us: swap_sum(): other = lax.ppermute(low, axis, [(0, 1), (1, 0)])]
    dot_general x7 -> x0, matrix products: 16.8 us -> none  [the longest x1 5.23 us: on_device(): jnp.einsum('qgjd,kgd->gjqk', d_mixed, value_group, preferred_element_type...]
    unnamed x99 -> x62, local copies, waits for them, and re-layouts: 26.8 us -> 12.4 us
    pallas_call x2 -> x0, local copies, waits for them, and re-layouts: 9.88 us -> none  [the longest x1 4.96 us: norm_gather(): pl.pallas_call(norm_kernel, out_shape=(jax.ShapeDtypeStruct((rows, width)...]
  transfers between devices with their start and end apart: 12 -> 4, of which waited for: 7 -> 1; matrix products, arithmetic and copies ran while one was open for 12% -> 11% of each run, Pallas kernels for 9% -> 14%
where the time goes in v3:
time: 375 us; the launch traced here: 368 us
  Pallas kernels  242 us (65%)
  matrix products  52.7 us (14%)
  local copies, waits for them, and re-layouts  33.6 us (9%)
  other arithmetic  18.3 us (5%)
  between operations  14.9 us (4%)
  starting transfers between devices  4.65 us (1%)
    pallas_call x1, Pallas kernels, layer_back(): pl.pallas_call(layer_back_kernel, out_shape=(jax.ShapeDtypeStruct((rows,...  150 us
    pallas_call x1, Pallas kernels, norm_gather(): pl.pallas_call(norm_kernel, out_shape=(jax.ShapeDtypeStruct((rows, width)...  51.6 us
    pallas_call x1, Pallas kernels, gather(): pl.pallas_call(gather_kernel, out_shape=(jax.ShapeDtypeStruct((16 * shard...  40.7 us
    dot_general x4, matrix products, tail_dot(): lax.dot_general(left, right, (((1,), (1,)), ((), ())), preferred_element_...  23.7 us
    unnamed x62, local copies, waits for them, and re-layouts  12.4 us
    dot_general x1, matrix products, on_device(): lift_lin = jnp.dot(normed_group, lift_full, preferred_element_type=f32)  8.84 us
  transfers between devices with their start and end apart: 4, of which 1 were waited for; matrix products, arithmetic and copies ran while one was open for 11% of the time, Pallas kernels for 14%

profile of v3, /device:TPU:0, one launch (start us, length us, event | category | flops | bytes accessed | tf_op | source)
XLA Modules:
  0.0 367.8 jit_solution(2161227147972857511)
XLA Ops:
  7.3 1.0 constant_dynamic-update-slice_fusion.3
  8.3 0.7 pad_maximum_fusion.4
  9.3 1.3 constant_dynamic-slice_fusion
  10.6 0.8 constant_dynamic-update-slice_fusion.2
  11.3 0.7 constant_dynamic-update-slice_fusion.1
  12.1 0.9 bitcast_dynamic-update-slice_fusion
  13.0 0.7 copy-done.16
  13.7 40.7 %gather_rows.1 = (bf16[1536,1920]{1,0:T(8,128)(2,1)}, bf16[1024,1536]{1,0:T(8,128)(2,1)}) custom-call(bf16[96,1920]{1,0:T(8,128)(2,1)} %copy-done.16, bf16[256,1536]{1,0:T(8,128)(2,1)} %dy_ref.1), custom_call_target="tpu_custom_call" | custom-call | tf_op jit(solution)/shard_map/gather_rows/pallas_call | solution.py:110
  54.4 0.9 pad_maximum_fusion
  55.3 0.2 reduce-window.8
  55.7 1.5 convert_reduce_fusion
  57.3 0.2 fusion.19
  57.5 0.3 fusion.21.normed_one_ref
  57.8 3.2 convolution_add_fusion
  61.0 0.5 multiply_cosine_fusion
  61.7 0.2 fusion.34
  61.9 0.8 pad_maximum_fusion.3
  62.6 3.0 collective-permute-start
  65.6 0.6 collective-permute-start.1
  66.3 1.0 collective-permute-start.2
  67.3 0.6 dynamic_slice.29
  68.0 0.3 copy.58
  68.5 0.3 copy.60
  69.0 0.3 copy.57
  69.4 1.1 fusion.25
  70.6 3.3 slice.132.out_hbm
  73.9 4.0 %slice.122.lin_hbm = bf16[1536,1024]{1,0:T(8,128)(2,1)} slice(bf16[1536,1920]{1,0:T(8,128)(2,1)} %get-tuple-element.26), slice={[0:1536], [0:1024]} | slice | bytes 6291456 | tf_op jit(solution)/shard_map/slice | solution.py:872
  77.9 0.6 reshape.209.gain_one_ref
  78.5 0.2 copy.61
  78.7 0.6 reshape.208.gain_ref.gain_two_ref
  79.3 0.9 constant_dynamic-update-slice_fusion.10
  80.2 0.9 constant_dynamic-update-slice_fusion.9
  81.1 0.9 constant_dynamic-update-slice_fusion.8
  82.1 0.9 constant_dynamic-update-slice_fusion.6
  83.0 0.9 constant_dynamic-update-slice_fusion.5
  84.0 0.9 constant_dynamic-update-slice_fusion.4
  84.9 1.4 fusion.2
  86.3 1.9 fusion.1
  88.2 2.5 fusion.22
  90.7 0.9 copy.64.mixed_ref
  91.6 3.8 %convolution_convert_fusion.1.part_ref = bf16[256,1536]{1,0:T(8,128)(2,1)} fusion(bf16[256,768]{0,1:T(8,128)(2,1)S(1)} %bitcast.112, bf16[1536,1920]{1,0:T(8,128)(2,1)} %get-tuple-element.26), kind=kOutput, calls=%fused_computation.26 | convolution fusion | flops 604372992 | bytes 3538944 | tf_op jit(solution)/shard_map/dot_general | solution.py:801
  95.4 51.6 %norm_gather.1 = (f32[256,1536]{1,0:T(8,128)}, bf16[1024,1536]{1,0:T(8,128)(2,1)}) custom-call(bf16[256,1536]{1,0:T(8,128)(2,1)} %convolution_convert_fusion.1.part_ref, bf16[256,1536]{1,0:T(8,128)(2,1)} %tokens_ref.1, f32[1,1536]{1,0:T(1,128)} %reshape.208.gain_ref.gain_two_ref), custom_call_target="tpu_custom_call" | custom-call | tf_op jit(solution)/shard_map/norm_gather/pallas_call | solution.py:165
  147.0 0.8 dynamic-slice_bitcast_fusion.1
  147.8 5.5 %fusion.7.probs_hbm = f32[6,256,1024]{2,1,0:T(8,128)} fusion(f32[6,256]{1,0:T(8,128)S(1)} %fusion.1, f32[6,256]{1,0:T(8,128)S(1)} %get-tuple-element.76, f32[1024,256,6]{0,1,2:T(8,128)} %copy-done.2, pred[256,1024]{1,0:T(8,128)(4,1)S(1)} %fusion.25), kind=kLoop, calls=%fused_computation.15 | loop fusion | flops 6291456 | bytes 12857344 | tf_op jit(solution)/shard_map/reshape | solution.py:922
  153.3 1.4 all-gather.2.cloned.1.call-done
  154.7 7.3 %fusion.11 = f32[1024,1152]{1,0:T(8,128)S(1)} fusion(bf16[1024,1536]{1,0:T(8,128)(2,1)} %get-tuple-element.27.normed_hbm, bf16[1536,3456]{1,0:T(8,128)(2,1)} %all-gather.2.cloned.1.call-done), kind=kOutput, calls=%fused_computation.18 | convolution fusion | flops 3623878656 | bytes 11403264 | tf_op jit(solution)/shard_map/dot_general | solution.py:908
  162.1 5.9 %fusion.17 = f32[1024,1152]{1,0:T(8,128)} fusion(bf16[1024,1536]{1,0:T(8,128)(2,1)S(1)} %copy-done.6, bf16[1536,3456]{1,0:T(8,128)(2,1)S(1)} %copy-done.23), kind=kOutput, calls=%fused_computation.24 | convolution fusion | flops 3623878656 | bytes 11403264 | tf_op jit(solution)/shard_map/dot_general | solution.py:907
  168.0 8.8 %select_convert_fusion = (bf16[1024,1152]{1,0:T(8,128)(2,1)S(1)}, bf16[1024,1152]{1,0:T(8,128)(2,1)S(1)}, bf16[1024,1152]{1,0:T(8,128)(2,1)S(1)}) fusion(pred[1152]{0:T(1024)(128)(4,1)S(1)} %iota_compare_fusion.2, f32[1024,1152]{1,0:T(8,128)S(1)} %fusion.11, f32[1024,1152]{1,0:T(8,128)} %fusion.17, bf16[1024,1536]{1,0:T(8,128)(2,1)S(1)} %copy-done.7, ...), kind=kOutput, calls=%fused_computation.6 | convolution fusion | flops 3645112320 | bytes 23201792 | tf_op jit(solution)/shard_map/dot_general | solution.py:909
  176.8 6.2 %fusion.9 = f32[1024,1536]{1,0:T(8,128)} fusion(bf16[1024,1152]{1,0:T(8,128)(2,1)S(1)} %get-tuple-element.41.gate_hbm, bf16[1536,3456]{1,0:T(8,128)(2,1)S(1)} %copy-done.23), kind=kOutput, calls=%fused_computation.16 | convolution fusion | flops 3623878656 | bytes 12189696 | tf_op jit(solution)/shard_map/dot_general | solution.py:801
  183.0 5.7 %convolution_convert_fusion.second_hbm = bf16[1024,1536]{1,0:T(8,128)(2,1)} fusion(bf16[1024,1152]{1,0:T(8,128)(2,1)S(1)} %get-tuple-element.40.hidden_hbm, bf16[1536,3456]{1,0:T(8,128)(2,1)S(1)} %copy-done.23), kind=kOutput, calls=%fused_computation.11 | convolution fusion | flops 3625451520 | bytes 9043968 | tf_op jit(solution)/shard_map/dot_general | solution.py:801
  188.7 8.0 %add_convert_fusion.first_hbm = bf16[1024,1536]{1,0:T(8,128)(2,1)} fusion(f32[1024,1536]{1,0:T(8,128)} %fusion.9, bf16[1024,1152]{1,0:T(8,128)(2,1)S(1)} %get-tuple-element.42.lift_hbm, bf16[1536,3456]{1,0:T(8,128)(2,1)S(1)} %copy-done.23), kind=kOutput, calls=%fused_computation.1 | convolution fusion | flops 3627024384 | bytes 15335424 | tf_op jit(solution)/shard_map/dot_general | solution.py:801
  196.7 150.0 %layer_back.1 = (bf16[256,1536]{1,0:T(8,128)(2,1)}, f32[256,1536]{1,0:T(8,128)}, f32[8,512]{1,0:T(8,128)}, f32[96,1792]{1,0:T(8,128)}, bf16[4,96,3456]{2,1,0:T(8,128)(2,1)}) custom-call(bf16[1024,1536]{1,0:T(8,128)(2,1)} %get-tuple-element.27.normed_hbm, bf16[1024,1536]{1,0:T(8,128)(2,1)} %get-tuple-element.28.dy_hbm, bf16[1024,1152]{1,0:T(8,128)(2,1)} %copy-done.9, ...), custom_call_target="tpu_custom_call" | custom-call | tf_op jit(solution)/shard_map/layer_back/pallas_call | solution.py:713
  346.7 1.9 slice_bitcast_fusion
  348.6 1.5 fusion.42
  350.0 0.7 slice_bitcast_fusion.15
  350.8 0.7 copy.67
  351.5 0.5 fusion.44
  352.0 2.1 slice_bitcast_fusion.4
  354.1 0.6 fusion.43
  354.7 1.3 maximum_convert_fusion
  356.1 1.3 maximum_convert_fusion.1
  357.4 1.3 convert_bitcast_fusion
  358.7 0.9 copy.82
  359.5 1.1 copy.83
  (78 shorter events, 1.5 us)
Async XLA Ops:
  7.2 2.0 copy-start
  7.2 48.1 %copy-start.22 = (s32[1,3]{1,0:T(1,128)S(1)}, s32[1,3]{1,0:T(1,128)}, u32[]{:S(2)}) copy-start(s32[1,3]{1,0:T(1,128)} %param.17) | copy-start | bytes 40
  7.2 48.5 %copy-start.20 = (bf16[128]{0:T(256)(128)(2,1)S(1)}, bf16[128]{0:T(256)(128)(2,1)}, u32[]{:S(2)}) copy-start(bf16[128]{0:T(256)(128)(2,1)} %param.24) | copy-start | bytes 772
  7.2 48.5 %copy-start.21 = (bf16[128]{0:T(256)(128)(2,1)S(1)}, bf16[128]{0:T(256)(128)(2,1)}, u32[]{:S(2)}) copy-start(bf16[128]{0:T(256)(128)(2,1)} %param.22) | copy-start | bytes 772
  7.2 48.5 %copy-start.19 = (bf16[768]{0:T(1024)(128)(2,1)S(1)}, bf16[768]{0:T(1024)(128)(2,1)}, u32[]{:S(2)}) copy-start(bf16[768]{0:T(1024)(128)(2,1)} %param.20) | copy-start | bytes 4612
  7.2 50.0 %copy-start.3 = (bf16[256,1536]{1,0:T(8,128)(2,1)S(1)}, bf16[256,1536]{1,0:T(8,128)(2,1)}, u32[]{:S(2)}) copy-start(bf16[256,1536]{1,0:T(8,128)(2,1)} %tokens_ref.1) | copy-start | bytes 2359300
  7.2 147.5 %all-gather.2.cloned.1.call-start = ((), (), s32[]{:S(2)}) async-start(), calls=%async_computation | async-start | bytes 11280384 | tf_op jit(solution)/shard_map/all_gather | solution.py:870
  13.0 0.7 copy-start.16
  55.6 11.7 %copy-start.17 = (s32[1024]{0:T(1024)}, s32[1024]{0:T(1024)S(1)}, u32[]{:S(2)}) copy-start(s32[1024]{0:T(1024)S(1)} %get-tuple-element.38) | copy-start | bytes 12292
  57.8 3.8 %copy-start.5 = (bf16[256,1536]{1,0:T(8,128)(2,1)}, bf16[256,1536]{1,0:T(8,128)(2,1)S(1)}, u32[]{:S(2)}) copy-start(bf16[256,1536]{1,0:T(8,128)(2,1)S(1)} %fusion.21.normed_one_ref) | copy-start | bytes 2359300
  61.9 6.7 %copy-start.13 = (f32[256,128]{1,0:T(8,128)}, f32[256,128]{1,0:T(8,128)S(1)}, u32[]{:S(2)}) copy-start(f32[256,128]{1,0:T(8,128)S(1)} %get-tuple-element.67.sin_ref) | copy-start | bytes 393220
  61.9 6.9 %copy-start.12 = (f32[256,128]{1,0:T(8,128)}, f32[256,128]{1,0:T(8,128)S(1)}, u32[]{:S(2)}) copy-start(f32[256,128]{1,0:T(8,128)S(1)} %get-tuple-element.66.cos_ref) | copy-start | bytes 393220
  62.6 16.6 %collective-permute-start = (bf16[256,2,128]{2,0,1:T(8,128)(2,1)}, bf16[256,2,128]{2,0,1:T(8,128)(2,1)}, u32[]{:S(2)}, u32[]{:S(2)}) collective-permute-start(bf16[256,2,128]{2,0,1:T(8,128)(2,1)} %get-tuple-element.63), channel_id=1, source_target_pairs={{0,6},{2,0},{4,2},{6,4},{1,7},{3,1},{5,3},{7,5},{8,14},{10,8},{12,... | collective-permute-start | bytes 393224 | tf_op jit(solution)/shard_map/ppermute | solution.py:809
  65.6 14.6 %collective-permute-start.1 = (bf16[256,2,128]{2,0,1:T(8,128)(2,1)}, bf16[256,2,128]{2,0,1:T(8,128)(2,1)}, u32[]{:S(2)}, u32[]{:S(2)}) collective-permute-start(bf16[256,2,128]{2,0,1:T(8,128)(2,1)} %get-tuple-element.63), channel_id=1, source_target_pairs={{0,4},{2,6},{4,0},{6,2},{1,5},{3,7},{5,1},{7,3},{8,12},{10,14},{12... | collective-permute-start | bytes 393224 | tf_op jit(solution)/shard_map/ppermute | solution.py:809
  66.3 14.9 %collective-permute-start.2 = (bf16[256,2,128]{2,0,1:T(8,128)(2,1)}, bf16[256,2,128]{2,0,1:T(8,128)(2,1)}, u32[]{:S(2)}, u32[]{:S(2)}) collective-permute-start(bf16[256,2,128]{2,0,1:T(8,128)(2,1)} %get-tuple-element.63), channel_id=1, source_target_pairs={{0,2},{2,4},{4,6},{6,0},{1,3},{3,5},{5,7},{7,1},{8,10},{10,12},{12... | collective-permute-start | bytes 393224 | tf_op jit(solution)/shard_map/ppermute | solution.py:809
  69.4 9.0 %copy-start.4 = (bf16[256,768]{1,0:T(8,128)(2,1)}, bf16[256,768]{1,0:T(8,128)(2,1)S(1)}, u32[]{:S(2)}) copy-start(bf16[256,768]{1,0:T(8,128)(2,1)S(1)} %add_convert_fusion.1.query_ref) | copy-start | bytes 1179652
  73.9 5.4 %copy-start.14 = (bf16[2048,2,128]{2,0,1:T(8,128)(2,1)S(1)}, bf16[2048,2,128]{2,0,1:T(8,128)(2,1)}, u32[]{:S(2)}) copy-start(bf16[2048,2,128]{2,0,1:T(8,128)(2,1)} %get-tuple-element.64) | copy-start | bytes 3145732
  86.3 4.4 %copy-start.2 = (f32[1024,256,6]{0,1,2:T(8,128)}, f32[1024,256,6]{0,1,2:T(8,128)S(1)}, u32[]{:S(2)}) copy-start(f32[1024,256,6]{0,1,2:T(8,128)S(1)} %get-tuple-element.77) | copy-start | bytes 18874372
  154.7 7.3 %copy-start.6 = (bf16[1024,1536]{1,0:T(8,128)(2,1)S(1)}, bf16[1024,1536]{1,0:T(8,128)(2,1)}, u32[]{:S(2)}) copy-start(bf16[1024,1536]{1,0:T(8,128)(2,1)} %get-tuple-element.28.dy_hbm) | copy-start | bytes 9437188
  154.7 7.3 %copy-start.23 = (bf16[1536,3456]{1,0:T(8,128)(2,1)S(1)}, bf16[1536,3456]{1,0:T(8,128)(2,1)}, u32[]{:S(2)}) copy-start(bf16[1536,3456]{1,0:T(8,128)(2,1)} %all-gather.2.cloned.1.call-done) | copy-start | bytes 31850500
  162.1 5.9 %copy-start.7 = (bf16[1024,1536]{1,0:T(8,128)(2,1)S(1)}, bf16[1024,1536]{1,0:T(8,128)(2,1)}, u32[]{:S(2)}) copy-start(bf16[1024,1536]{1,0:T(8,128)(2,1)} %get-tuple-element.27.normed_hbm) | copy-start | bytes 9437188
  176.8 6.2 %copy-start.9 = (bf16[1024,1152]{1,0:T(8,128)(2,1)}, bf16[1024,1152]{1,0:T(8,128)(2,1)S(1)}, u32[]{:S(2)}) copy-start(bf16[1024,1152]{1,0:T(8,128)(2,1)S(1)} %get-tuple-element.41.gate_hbm) | copy-start | bytes 7077892
  176.8 6.2 %copy-start.8 = (bf16[1024,1152]{1,0:T(8,128)(2,1)}, bf16[1024,1152]{1,0:T(8,128)(2,1)S(1)}, u32[]{:S(2)}) copy-start(bf16[1024,1152]{1,0:T(8,128)(2,1)S(1)} %get-tuple-element.40.hidden_hbm) | copy-start | bytes 7077892
  176.8 11.9 %copy-start.10 = (bf16[1024,1152]{1,0:T(8,128)(2,1)}, bf16[1024,1152]{1,0:T(8,128)(2,1)S(1)}, u32[]{:S(2)}) copy-start(bf16[1024,1152]{1,0:T(8,128)(2,1)S(1)} %get-tuple-element.42.lift_hbm) | copy-start | bytes 7077892
  351.5 4.6 %copy-start.18 = (f32[1,4,2,128]{3,1,2,0:T(4,128)}, f32[1,4,2,128]{3,1,2,0:T(4,128)S(1)}, u32[]{:S(2)}) copy-start(f32[1,4,2,128]{3,1,2,0:T(4,128)S(1)} %copy.68) | copy-start | bytes 12292
  354.7 3.9 %copy-start.15 = (bf16[256,1536]{1,0:T(8,128)(2,1)S(1)}, bf16[256,1536]{1,0:T(8,128)(2,1)}, u32[]{:S(2)}) copy-start(bf16[256,1536]{1,0:T(8,128)(2,1)} %get-tuple-element.94) | copy-start | bytes 2359300
  356.1 3.5 copy-start.11
  357.4 3.3 copy-start.1
Sparse Core Ops, SparseCore 0:
  55.4 99.2 all-gather.1
